TPU v7x, 256 devices: a whole 4x4x8 slice. The times are simulated.
256 devices in a mesh: lat: 16 (over z, y_lo), mp: 16 (over y_hi, x, core).
Axes of the slice: x: 4, y: 4 (y_hi: 2, y_lo: 2; y = y_hi * 2 + y_lo), z: 8, core: 2. Of those that a mesh axis runs over, the one named last changes fastest.
Arguments:
- tokens: bfloat16 [32768, 1024], P(('lat', 'mp')), may hold values from -20 to 20
- gain: float32 [1024], replicated, may hold values from 0.1 to 1.9
- qkv_weight: bfloat16 [16, 192, 1024], P('mp'), may hold values from -2 to 2
- out_weight: bfloat16 [16, 64, 1024], P('mp'), may hold values from -1 to 1
- row_cells: int32 [128], replicated, may hold values from 32 to 256, as said below
- upstream: bfloat16 [32768, 1024], P(('lat', 'mp')), may hold values from -6 to 6
Outputs:
- update: bfloat16 [32768, 1024], P(('lat', 'mp'))
- grad_input: bfloat16 [32768, 1024], P(('lat', 'mp'))
- grad_qkv: float32 [16, 192, 1024], P('mp')
- grad_out: float32 [16, 64, 1024], P('mp')
Inputs may be any that keep to these rules, and one draw needn't show every extreme that they name: `row_cells`: A row's live cells are its first ones; rows at the equator hold all 256, rows at the poles 256 // 8.
All inputs are finite; a program needn't handle non-finite values.
Results may differ from a plain program's by a relative error of at most 0.0085.
The roundings to bfloat16 on the way count: a program that leaves them out, or rounds other values in their place, can miss the bound.
Values may be sent and summed in bfloat16 or wider, within the bound.
A program may use at most 64 MiB of HBM per device.

v0:
```python
import math

import jax
import jax.numpy as jnp
from jax import lax
from jax.sharding import PartitionSpec as P

WIDTH = 1024
HEAD_WIDTH = 64
LONGITUDES = 256
BAND_ROWS = 8


def padded(x, sides, width):
    for axis, dim in sides:
        size, length = (lax.axis_size(axis), x.shape[dim])
        up = [(i, (i + 1) % size) for i in range(size - 1)]
        down = [(j, i) for i, j in up]
        last = lax.slice_in_dim(x, length - width, length, axis=dim)
        initial = lax.slice_in_dim(x, 0, width, axis=dim)
        before = lax.ppermute(last, axis, up)
        after = lax.ppermute(initial, axis, down)
        x = jnp.concatenate([before, x, after], axis=dim)
    return x


def passed_along(x, axis, by):
    length = lax.axis_size(axis)
    pairs = [(i, i + by) for i in range(length) if 0 <= i + by < length]
    return lax.ppermute(x, axis, pairs)


def tile_mask(row_start, col_start, cells_pad, col_tile, key_cols):
    query_rows = jnp.arange(4, dtype=jnp.int32)
    key_rows = jnp.arange(16, dtype=jnp.int32)
    query_cols = col_start + jnp.arange(col_tile, dtype=jnp.int32)
    key_index = (col_start - 8 + jnp.arange(key_cols, dtype=jnp.int32)) % LONGITUDES
    query_cells = lax.dynamic_slice_in_dim(cells_pad, row_start + 6, 4)
    key_cells = lax.dynamic_slice_in_dim(cells_pad, row_start, 16)
    query_live = query_cols[None, :] < query_cells[:, None]
    key_live = key_index[None, :] < key_cells[:, None]
    row_near = jnp.abs(key_rows[None, :] - 6 - query_rows[:, None]) <= 6
    offset = (key_index[None, :] - query_cols[:, None]) % LONGITUDES
    col_near = (offset <= 6) | (offset >= LONGITUDES - 6)
    allowed = (
        query_live[:, :, None, None]
        & key_live[None, None, :, :]
        & row_near[:, None, :, None]
        & col_near[None, :, None, :]
    )
    return (
        allowed.reshape(4 * col_tile, 16 * key_cols),
        query_live.reshape(4 * col_tile),
        key_index,
    )


def tile_probs(queries, keys_tile, allowed, query_live, score_scale):
    scores = (
        jnp.einsum("qhd,khd->hqk", queries, keys_tile, preferred_element_type=jnp.float32)
        * score_scale
    )
    masked = jnp.where(allowed[None], scores, -1e30)
    highest = jnp.max(masked, axis=2, keepdims=True)
    terms = jnp.where(allowed[None], jnp.exp(masked - highest), 0.0)
    total = (
        jnp.sum(terms, axis=2, keepdims=True)
        + (1.0 - query_live.astype(jnp.float32))[None, :, None]
    )
    return terms / total


def assemble(tiles, row_total, col_tile, heads, width):
    layout = tiles.reshape(row_total // 4, LONGITUDES // col_tile, 4, col_tile, heads, width)
    return layout.transpose(0, 2, 1, 3, 4, 5).reshape(row_total * LONGITUDES, heads * width)


def on_device(tokens, gain, qkv_weight, out_weight, row_cells, upstream):
    local_heads = qkv_weight.shape[0]
    band_tokens = BAND_ROWS * LONGITUDES
    score_scale = 1.0 / math.sqrt(HEAD_WIDTH)
    grad_scale = 4.0 / math.sqrt(band_tokens * lax.axis_size("lat"))
    band_start = lax.axis_index("lat") * BAND_ROWS
    col_tile = min(128, LONGITUDES)
    key_cols = min(LONGITUDES, col_tile + 16)
    col_tiles = LONGITUDES // col_tile
    tile_count = BAND_ROWS // 4 * col_tiles
    zero_index = jnp.zeros((), jnp.int32)
    features = tokens.astype(jnp.float32)
    inverse = lax.rsqrt(jnp.mean(features * features, axis=1, keepdims=True) + 1e-06)
    normed = (features * inverse * gain[None, :]).astype(jnp.bfloat16)
    normed_band = lax.all_gather(normed, "mp", axis=0, tiled=True)
    qkv_band = jnp.einsum(
        "td,hed->the", normed_band, qkv_weight, preferred_element_type=jnp.float32
    ).astype(jnp.bfloat16)
    qkv_grid = qkv_band.reshape(BAND_ROWS, LONGITUDES, local_heads, 3 * HEAD_WIDTH)
    queries_all = qkv_grid[..., :HEAD_WIDTH]
    keyval_ext = padded(qkv_grid[..., HEAD_WIDTH:], (("lat", 0),), 6)
    cells_pad = jnp.pad(row_cells, (6, 6))

    def tile_anchor(tile_index):
        return (tile_index // col_tiles * 4, tile_index % col_tiles * col_tile)

    def tile_inputs(tile_index):
        row_start, col_start = tile_anchor(tile_index)
        allowed, query_live, key_index = tile_mask(
            band_start + row_start, col_start, cells_pad, col_tile, key_cols
        )
        queries = lax.dynamic_slice(
            queries_all,
            (row_start, col_start, zero_index, zero_index),
            (4, col_tile, local_heads, HEAD_WIDTH),
        ).reshape(4 * col_tile, local_heads, HEAD_WIDTH)
        key_block = jnp.take(
            lax.dynamic_slice_in_dim(keyval_ext, row_start, 16, 0), key_index, axis=1
        )
        key_block = key_block.reshape(16 * key_cols, local_heads, 2 * HEAD_WIDTH)
        return (allowed, query_live, key_index, queries, key_block)

    def forward_tile(tile_index):
        allowed, query_live, key_index, queries, key_block = tile_inputs(tile_index)
        probabilities = tile_probs(
            queries, key_block[..., :HEAD_WIDTH], allowed, query_live, score_scale
        )
        weights = probabilities.astype(jnp.bfloat16)
        return jnp.einsum(
            "hqk,khd->qhd", weights, key_block[..., HEAD_WIDTH:], preferred_element_type=jnp.float32
        ).astype(jnp.bfloat16)

    tile_ids = jnp.arange(tile_count, dtype=jnp.int32)
    heads_out = assemble(
        lax.map(forward_tile, tile_ids), BAND_ROWS, col_tile, local_heads, HEAD_WIDTH
    )
    out_flat = out_weight.reshape(local_heads * HEAD_WIDTH, WIDTH)
    token_part = heads_out
    update = lax.psum_scatter(
        jnp.dot(token_part, out_flat, preferred_element_type=jnp.float32),
        "mp",
        scatter_dimension=0,
        tiled=True,
    ).astype(jnp.bfloat16)
    band_upstream = lax.all_gather(upstream, "mp", axis=0, tiled=True)
    grad_heads = lax.dot_general(
        band_upstream, out_flat, (((1,), (1,)), ((), ())), preferred_element_type=jnp.float32
    ).astype(jnp.bfloat16)
    grad_out_part = lax.dot_general(
        heads_out, band_upstream, (((0,), (0,)), ((), ())), preferred_element_type=jnp.float32
    )
    grad_grid = grad_heads.reshape(BAND_ROWS, LONGITUDES, local_heads, HEAD_WIDTH)

    def backward_tile(key_accum, tile_index):
        allowed, query_live, key_index, queries, key_block = tile_inputs(tile_index)
        row_start, col_start = tile_anchor(tile_index)
        grad_tile = lax.dynamic_slice(
            grad_grid,
            (row_start, col_start, zero_index, zero_index),
            (4, col_tile, local_heads, HEAD_WIDTH),
        ).reshape(4 * col_tile, local_heads, HEAD_WIDTH)
        keys_tile = key_block[..., :HEAD_WIDTH]
        values_tile = key_block[..., HEAD_WIDTH:]
        probabilities = tile_probs(queries, keys_tile, allowed, query_live, score_scale)
        weights = probabilities.astype(jnp.bfloat16)
        grad_probs = jnp.einsum(
            "qhd,khd->hqk", grad_tile, values_tile, preferred_element_type=jnp.float32
        )
        row_delta = jnp.sum(probabilities * grad_probs, axis=2, keepdims=True)
        grad_scores = (probabilities * (grad_probs - row_delta)).astype(jnp.bfloat16)
        grad_query = (
            jnp.einsum("hqk,khd->qhd", grad_scores, keys_tile, preferred_element_type=jnp.float32)
            * score_scale
        ).astype(jnp.bfloat16)
        grad_key = (
            jnp.einsum("hqk,qhd->khd", grad_scores, queries, preferred_element_type=jnp.float32)
            * score_scale
        )
        grad_value = jnp.einsum(
            "hqk,qhd->khd", weights, grad_tile, preferred_element_type=jnp.float32
        )
        key_grads = jnp.concatenate([grad_key, grad_value], axis=2).reshape(
            16, key_cols, local_heads, 2 * HEAD_WIDTH
        )
        key_grads, grad_query = (key_grads, grad_query)
        rows_hit = row_start + jnp.arange(16, dtype=jnp.int32)
        key_accum = key_accum.at[rows_hit[:, None], key_index[None, :]].add(key_grads)
        return (key_accum, grad_query)

    accum_start = jnp.zeros((BAND_ROWS + 12, LONGITUDES, local_heads, 2 * HEAD_WIDTH), jnp.float32)
    key_accum, query_tiles = lax.scan(backward_tile, accum_start, tile_ids)
    from_above = passed_along(key_accum[:6], "lat", -1)
    from_below = passed_along(key_accum[BAND_ROWS + 6 :], "lat", 1)
    own_rows = key_accum[6 : BAND_ROWS + 6]
    own_rows = own_rows.at[:6].add(from_below).at[BAND_ROWS - 6 :].add(from_above)
    grad_keyval = own_rows.astype(jnp.bfloat16).reshape(band_tokens, local_heads, 2 * HEAD_WIDTH)
    grad_query_all = assemble(query_tiles, BAND_ROWS, col_tile, local_heads, HEAD_WIDTH)
    grad_query_all = grad_query_all.reshape(band_tokens, local_heads, HEAD_WIDTH)
    grad_proj = jnp.concatenate([grad_query_all, grad_keyval], axis=2)
    grad_qkv_part = jnp.einsum(
        "the,td->hed", grad_proj, normed_band, preferred_element_type=jnp.float32
    )
    grad_qkv, grad_out = lax.psum((grad_qkv_part, grad_out_part), "lat")
    token_part = grad_proj
    grad_normed = lax.psum_scatter(
        jnp.einsum("the,hed->td", token_part, qkv_weight, preferred_element_type=jnp.float32),
        "mp",
        scatter_dimension=0,
        tiled=True,
    )
    centred = features * inverse
    scaled = gain[None, :] * grad_normed
    grad_input = inverse * (scaled - centred * jnp.mean(scaled * centred, axis=1, keepdims=True))
    return (
        update,
        grad_input.astype(jnp.bfloat16),
        grad_qkv * grad_scale,
        (grad_out * grad_scale).reshape(local_heads, HEAD_WIDTH, WIDTH),
    )


def solution(mesh):
    return jax.shard_map(
        on_device,
        mesh=mesh,
        in_specs=(
            P(("lat", "mp"), None),
            P(),
            P("mp", None, None),
            P("mp", None, None),
            P(),
            P(("lat", "mp"), None),
        ),
        out_specs=(
            P(("lat", "mp"), None),
            P(("lat", "mp"), None),
            P("mp", None, None),
            P("mp", None, None),
        ),
        check_vma=False,
    )
```

profile of v0, /device:TPU:2, one launch (start us, length us, event | category | flops | bytes accessed | tf_op | source)
XLA Modules:
  0.0 846.6 jit_solution(8454119843018144857)
XLA Ops:
  11.0 64.2 %all-gather.3.cloned.1.call-done = bf16[2048,1024]{1,0:T(8,128)(2,1)} async-done(((bf16[128,1024]{1,0:T(8,128)(2,1)}), bf16[2048,1024]{1,0:T(8,128)(2,1)}) %all-gather.3.cloned.1.call-update) | async-done | bytes 4194320 | tf_op jit(solution)/shard_map/all_gather | solution.py:92
  75.2 3.7 convolution_convert_fusion
  82.0 4.6 collective-permute-start
  86.7 59.0 %all-gather.5.cloned.1.call-done = bf16[2048,1024]{1,0:T(8,128)(2,1)} async-done(((bf16[128,1024]{1,0:T(8,128)(2,1)}), bf16[2048,1024]{1,0:T(8,128)(2,1)}) %all-gather.5.cloned.1.call-update) | async-done | bytes 4194320 | tf_op jit(solution)/shard_map/all_gather | solution.py:142
  145.8 3.6 convolution_convert_fusion.1
  153.3 196.2 %while.31 = (s32[]{:T(128)}, f32[20,256,1,128]{3,1,0,2:T(8,128)S(1)}, bf16[4,512,1,64]{1,3,2,0:T(8,128)(2,1)}, s32[4]{0:T(128)S(1)}, bf16[8,256,1,64]{1,0,3,2:T(...) while((s32[]{:T(128)}, ...), condition=%wide.region_11.13_spmd, body=%wide.region_6.12_spmd.sunk | while | flops 784704576 | bytes 83502104 | solution.py:188
  162.0 2.8 gather_fusion.1
  173.2 2.1 fusion.93
  175.5 2.5 multiply_reduce_fusion.2
  182.1 2.7 copy.152
  184.8 15.5 %scatter_fusion = f32[5120,128]{1,0:T(8,128)S(1)} fusion(f32[5120,128]{1,0:T(8,128)S(1)} %bitcast.293, s32[2304]{0:T(1024)S(1)} %reshape.795, f32[2304,128]{1,0:T(8,128)} %copy.152), kind=kCustom, calls=%fused_computation.2.clone.1 | custom fusion | flops 294912 | bytes 3548160 | tf_op jit(solution)/shard_map/while
  208.8 2.8 gather_fusion.1
  220.0 2.1 fusion.93
  222.2 2.5 multiply_reduce_fusion.2
  228.9 2.7 copy.152
  231.5 15.5 %scatter_fusion = f32[5120,128]{1,0:T(8,128)S(1)} fusion(f32[5120,128]{1,0:T(8,128)S(1)} %bitcast.293, s32[2304]{0:T(1024)S(1)} %reshape.795, f32[2304,128]{1,0:T(8,128)} %copy.152), kind=kCustom, calls=%fused_computation.2.clone.1 | custom fusion | flops 294912 | bytes 3548160 | tf_op jit(solution)/shard_map/while
  255.5 2.8 gather_fusion.1
  266.7 2.1 fusion.93
  268.9 2.5 multiply_reduce_fusion.2
  275.6 2.7 copy.152
  278.3 15.5 %scatter_fusion = f32[5120,128]{1,0:T(8,128)S(1)} fusion(f32[5120,128]{1,0:T(8,128)S(1)} %bitcast.293, s32[2304]{0:T(1024)S(1)} %reshape.795, f32[2304,128]{1,0:T(8,128)} %copy.152), kind=kCustom, calls=%fused_computation.2.clone.1 | custom fusion | flops 294912 | bytes 3548160 | tf_op jit(solution)/shard_map/while
  302.2 2.8 gather_fusion.1
  313.5 2.1 fusion.93
  315.7 2.5 multiply_reduce_fusion.2
  322.3 2.7 copy.152
  325.0 15.5 %scatter_fusion = f32[5120,128]{1,0:T(8,128)S(1)} fusion(f32[5120,128]{1,0:T(8,128)S(1)} %bitcast.293, s32[2304]{0:T(1024)S(1)} %reshape.795, f32[2304,128]{1,0:T(8,128)} %copy.152), kind=kCustom, calls=%fused_computation.2.clone.1 | custom fusion | flops 294912 | bytes 3548160 | tf_op jit(solution)/shard_map/while
  352.0 5.5 collective-permute-start.2
  358.2 93.0 %while.30 = (s32[]{:T(128)}, bf16[4,512,1,64]{1,3,2,0:T(8,128)(2,1)}, s32[4]{0:T(128)S(1)}, bf16[20,256,1,128]{3,1,0,2:T(8,128)(2,1)}, s32[]{:T(128)}, /*index=5...) while((s32[]{:T(128)}, ...), condition=%wide.region_4.6_spmd, body=%wide.region_1.5_spmd.sunk | while | flops 325017344 | bytes 42356512 | solution.py:132
  365.1 2.8 gather_fusion
  376.3 2.1 fusion.83
  378.5 3.0 fusion.84
  388.3 2.8 gather_fusion
  399.6 2.1 fusion.83
  401.8 3.0 fusion.84
  411.5 2.8 gather_fusion
  422.8 2.1 fusion.83
  425.0 3.0 fusion.84
  434.8 2.8 gather_fusion
  446.0 2.1 fusion.83
  448.3 3.0 fusion.84
  458.8 3.8 fusion.59
  466.5 2.1 convolution_bitcast_fusion.1
  468.7 4.5 fusion.50
  473.2 4.5 fusion.37
  477.8 129.5 %all-reduce.4.cloned.1.call-done = (f32[1,192,1024]{2,1,0:T(8,128)}, f32[64,1024]{1,0:T(8,128)}) async-done(((f32[1,192,1024]{2,1,0:T(8,128)}, f32[64,1024]{1,0:T(8,128)}), (f32[1,192,1024]{2,1,0:T(8,128)}, f32[64,1024]{1,0:T(8,128)})) %all-reduce.4.cloned.1.call-update) | async-done | bytes 1048592 | tf_op jit(solution)/shard_map/psum | solution.py:200
  609.0 2.2 broadcast_multiply_fusion
  611.1 111.2 %reduce-scatter.3.cloned.1.call-done = f32[128,1024]{1,0:T(8,128)} async-done(((f32[2048,1024]{1,0:T(8,128)}), f32[128,1024]{1,0:T(8,128)}) %reduce-scatter.3.cloned.1.call-update) | async-done | bytes 524304 | tf_op jit(solution)/shard_map/reduce_scatter | solution.py:136
  724.1 112.6 %reduce-scatter.5.cloned.1.call-done = f32[128,1024]{1,0:T(8,128)} async-done(((f32[2048,1024]{1,0:T(8,128)}), f32[128,1024]{1,0:T(8,128)}) %reduce-scatter.5.cloned.1.call-update) | async-done | bytes 524304 | tf_op jit(solution)/shard_map/reduce_scatter | solution.py:202
  (366 shorter events, 156.7 us)
Async XLA Ops:
  7.2 68.0 %copy-start = (bf16[1,192,1024]{2,1,0:T(8,128)(2,1)S(1)}, bf16[1,192,1024]{2,1,0:T(8,128)(2,1)}, u32[]{:S(2)}) copy-start(bf16[1,192,1024]{2,1,0:T(8,128)(2,1)} %param.18) | copy-start | bytes 1179652
  7.2 68.0 %all-gather.3.cloned.1.call-start = ((), (), s32[]{:S(2)}) async-start(), calls=%async_computation.2 | async-start | bytes 4456448 | tf_op jit(solution)/shard_map/all_gather | solution.py:92
  8.4 70.5 %copy-start.10 = (f32[128]{0:T(128)}, f32[128]{0:T(128)S(1)}, u32[]{:S(2)}) copy-start(f32[128]{0:T(128)S(1)} %add_rsqrt_fusion) | copy-start | bytes 1540
  10.2 135.6 %all-gather.5.cloned.1.call-start = ((), (), s32[]{:S(2)}) async-start(), calls=%async_computation.4 | async-start | bytes 4456448 | tf_op jit(solution)/shard_map/all_gather | solution.py:142
  10.9 596.3 %all-reduce.4.cloned.1.call-start = ((), (), s32[]{:S(2)}) async-start(), calls=%async_computation.6 | async-start | bytes 2097152 | tf_op jit(solution)/shard_map/psum | solution.py:200
  79.3 7.3 copy-start.12
  79.6 66.1 %copy-start.5 = (bf16[1,64,1024]{2,1,0:T(8,128)(2,1)S(1)}, bf16[1,64,1024]{2,1,0:T(8,128)(2,1)}, u32[]{:S(2)}) copy-start(bf16[1,64,1024]{2,1,0:T(8,128)(2,1)} %param.19) | copy-start | bytes 393220
  80.7 69.8 %collective-permute-start.1 = (bf16[6,256,1,128]{3,1,0,2:T(8,128)(2,1)}, bf16[6,256,1,128]{3,1,0,2:T(8,128)(2,1)S(1)}, u32[]{:S(2)}, u32[]{:S(2)}) collective-permute-start(bf16[6,256,1,128]{3,1,0,2:T(8,128)(2,1)} %copy.69), channel_id=1, source_target_pairs={{16,0},{32,16},{48,32},{64,48},{80,64},{96,80},{112,96},{128,112},... | collective-permute-start | bytes 1179656 | tf_op jit(solution)/shard_map/ppermute | solution.py:22
  82.0 68.5 %collective-permute-start = (bf16[6,256,1,128]{3,1,0,2:T(8,128)(2,1)S(1)}, bf16[6,256,1,128]{3,1,0,2:T(8,128)(2,1)S(1)}, u32[]{:S(2)}, u32[]{:S(2)}) collective-permute-start(bf16[6,256,1,128]{3,1,0,2:T(8,128)(2,1)S(1)} %copy.67), channel_id=1, source_target_pairs={{0,16},{16,32},{32,48},{48,64},{64,80},{80,96},{96,112},{112,128},... | collective-permute-start | bytes 1179656 | tf_op jit(solution)/shard_map/ppermute | solution.py:21
  152.6 0.7 copy-start.8
  152.6 0.7 copy-start.9
  350.8 113.3 %collective-permute-start.3 = (f32[6,256,1,128]{3,1,0,2:T(8,128)}, f32[6,256,1,128]{3,1,0,2:T(8,128)}, u32[]{:S(2)}, u32[]{:S(2)}) collective-permute-start(f32[6,256,1,128]{3,1,0,2:T(8,128)} %get-tuple-element.377), channel_id=1, source_target_pairs={{16,0},{32,16},{48,32},{64,48},{80,64},{96,80},{112,96},{128,112},... | collective-permute-start | bytes 2359304 | tf_op jit(solution)/shard_map/ppermute | solution.py:30
  352.0 110.6 %collective-permute-start.2 = (f32[6,256,1,128]{3,1,0,2:T(8,128)}, f32[6,256,1,128]{3,1,0,2:T(8,128)}, u32[]{:S(2)}, u32[]{:S(2)}) collective-permute-start(f32[6,256,1,128]{3,1,0,2:T(8,128)} %get-tuple-element.378), channel_id=1, source_target_pairs={{0,16},{16,32},{32,48},{48,64},{64,80},{80,96},{96,112},{112,128},... | collective-permute-start | bytes 2359304 | tf_op jit(solution)/shard_map/ppermute | solution.py:30
  451.2 1.1 copy-start.4
  458.8 3.8 copy-start.1
  462.6 2.9 copy-start.13
  465.5 1.0 copy-start.3
  466.5 2.2 copy-start.6
  468.6 253.7 %reduce-scatter.3.cloned.1.call-start = ((), (), s32[]{:S(2)}) async-start(), calls=%async_computation.3 | async-start | bytes 8912896 | tf_op jit(solution)/shard_map/reduce_scatter | solution.py:136
  473.2 363.5 %reduce-scatter.5.cloned.1.call-start = ((), (), s32[]{:S(2)}) async-start(), calls=%async_computation.5 | async-start | bytes 8912896 | tf_op jit(solution)/shard_map/reduce_scatter | solution.py:202
  609.0 227.7 %copy-start.2 = (bf16[128,1024]{1,0:T(8,128)(2,1)S(1)}, bf16[128,1024]{1,0:T(8,128)(2,1)}, u32[]{:S(2)}) copy-start(bf16[128,1024]{1,0:T(8,128)(2,1)} %param.16) | copy-start | bytes 786436
  609.0 227.7 %copy-start.7 = (f32[1024]{0:T(1024)S(1)}, f32[1024]{0:T(1024)}, u32[]{:S(2)}) copy-start(f32[1024]{0:T(1024)} %param.17) | copy-start | bytes 12292
  609.0 227.7 %copy-start.11 = (f32[128]{0:T(128)S(1)}, f32[128]{0:T(128)}, u32[]{:S(2)}) copy-start(f32[128]{0:T(128)} %copy-done.10) | copy-start | bytes 1540
Sparse Core Ops, SparseCore 0:
  11.3 63.8 all-gather.2
  77.9 67.8 all-gather.4
  468.7 138.5 all-reduce.3
  612.4 109.8 reduce-scatter.2
  727.5 109.1 reduce-scatter.4
where the time goes:
time: 853 us; the launch traced here: 847 us
  waiting for transfers between devices  477 us (56%)
  local copies, waits for them, and re-layouts  127 us (15%)
  other arithmetic  116 us (14%)
  matrix products  69.7 us (8%)
  loops' own time  30.6 us (4%)
  between operations  14.2 us (2%)
  starting transfers between devices  12.8 us (2%)
    psum x1, waiting for transfers between devices, on_device(): grad_qkv, grad_out = lax.psum((grad_qkv_part, grad_out_part), 'lat')  130 us
    reduce_scatter x1, waiting for transfers between devices, on_device(): lax.psum_scatter(jnp.einsum('the,hed->td', token_part, qkv_weight, prefer...  113 us
    reduce_scatter x1, waiting for transfers between devices, on_device(): lax.psum_scatter(jnp.dot(token_part, out_flat, preferred_element_type=jnp...  111 us
    all_gather x1, waiting for transfers between devices, on_device(): normed_band = lax.all_gather(normed, 'mp', axis=0, tiled=True)  64.2 us
    while x16, other arithmetic  62.8 us
    all_gather x1, waiting for transfers between devices, on_device(): band_upstream = lax.all_gather(upstream, 'mp', axis=0, tiled=True)  59 us
    and x32, local copies, waits for them, and re-layouts, tile_mask(): query_live[:, :, None, None] & key_live[None, None, :, :]  30.9 us
    another operation x16, local copies, waits for them, and re-layouts, tile_inputs(): jnp.take(lax.dynamic_slice_in_dim(keyval_ext, row_start, 16, 0), key_inde...  23.7 us
  transfers between devices with their start and end apart: 9, of which 5 were waited for; matrix products, arithmetic and copies ran while one was open for 14% of the time, Pallas kernels for 0%

commit v1 on v0

v1 whole, which is shorter than its diff:
```python
import math

import jax
import jax.numpy as jnp
from jax import lax
from jax.experimental import pallas as pl
from jax.experimental.pallas import tpu as pltpu
from jax.sharding import PartitionSpec as P

WIDTH = 1024
HEAD_WIDTH = 64
LONGITUDES = 256
BAND_ROWS = 8
REACH = 6
KEY_ROWS = BAND_ROWS + 2 * REACH
TILE = 16
WINDOW = 2 * TILE
TILES = LONGITUDES // TILE
KEY_COLS = LONGITUDES + TILE
QUERY_COLS = LONGITUDES + TILE // 2
NEVER = -1e30
VMEM = pltpu.VMEM


def passed_along(x, axis, by):
    length = lax.axis_size(axis)
    pairs = [(i, i + by) for i in range(length) if 0 <= i + by < length]
    return lax.ppermute(x, axis, pairs)


def key_features(cells):
    shape = (KEY_ROWS, KEY_COLS, 128)
    row = lax.broadcasted_iota(jnp.int32, shape, 0)
    col = lax.broadcasted_iota(jnp.int32, shape, 1)
    lane = lax.broadcasted_iota(jnp.int32, shape, 2)
    live = col % LONGITUDES < cells[:, None, None]
    near_row = (row >= lane - 8) & (row <= lane - 8 + 2 * REACH)
    apart = (col - lane) % 32
    near_col = (apart <= REACH) | (apart >= 32 - REACH)
    barred = (
        ((lane == 0) & ~live)
        | ((lane >= 8) & (lane < 16) & ~near_row)
        | ((lane >= 32) & (lane < 64) & ~near_col)
    )
    return jnp.where(barred, NEVER, 0.0).astype(jnp.bfloat16)


def query_features():
    shape = (2, BAND_ROWS, TILE, 128)
    tile, row, col, lane = (lax.broadcasted_iota(jnp.int32, shape, d) for d in range(4))
    picked = (
        (lane == 0)
        | (lane == 8 + row)
        | (lane == 32 + (TILE * tile + TILE // 2 + col) % 32)
    )
    return picked.astype(jnp.bfloat16).reshape(2, BAND_ROWS * TILE, 128)


def live_queries(cells):
    shape = (TILES, 1, BAND_ROWS, TILE)
    tile, _, _, col = (lax.broadcasted_iota(jnp.int32, shape, d) for d in range(4))
    at = (TILE * tile + TILE // 2 + col) % LONGITUDES
    live = at < cells[REACH : REACH + BAND_ROWS][None, None, :, None]
    return live.astype(jnp.float32).reshape(TILES, 1, BAND_ROWS * TILE)


def attention_tile(i, kv_ref, feat_ref, q_ref, g_ref, pick_ref, live_ref, oq_ref, dkv_ref):
    queries = BAND_ROWS * TILE
    keys = KEY_ROWS * WINDOW
    c0 = pl.multiple_of(i * TILE, TILE)
    at = pl.multiple_of(i * TILE + TILE // 2, TILE // 2)
    kv = kv_ref[:, pl.ds(c0, WINDOW), :].reshape(keys, 128)
    feat = feat_ref[:, pl.ds(c0, WINDOW), :].reshape(keys, 128)
    q = q_ref[:, pl.ds(at, TILE), :].reshape(queries, 128).astype(jnp.bfloat16)
    g = g_ref[:, pl.ds(at, TILE), :].reshape(queries, 128).astype(jnp.bfloat16)
    pick = pick_ref[lax.rem(i, 2)]
    both = jnp.concatenate(
        [
            jnp.concatenate([q, pick], axis=1),
            jnp.concatenate([g, jnp.zeros_like(g)], axis=1),
        ],
        axis=0,
    )
    products = lax.dot_general(
        jnp.concatenate([kv, feat], axis=1),
        both,
        (((1,), (1,)), ((), ())),
        preferred_element_type=jnp.float32,
    )
    scores = products[:, :queries]
    grad_probs = products[:, queries:]
    highest = jnp.max(scores, axis=0, keepdims=True)
    terms = jnp.exp(scores - highest)
    probs = terms * (live_ref[i] / jnp.sum(terms, axis=0, keepdims=True))
    weights = probs.astype(jnp.bfloat16)
    row_delta = jnp.sum(probs * grad_probs, axis=0, keepdims=True)
    grad_scores = (probs * (grad_probs - row_delta)).astype(jnp.bfloat16)
    pair = jnp.concatenate([weights, grad_scores], axis=1)
    dkv = jnp.dot(pair, jnp.concatenate([g, q], axis=0), preferred_element_type=jnp.float32)
    dkv_ref[:, pl.ds(c0, WINDOW), :] += dkv.reshape(KEY_ROWS, WINDOW, 128)
    out = lax.dot_general(
        pair, kv, (((0,), (0,)), ((), ())), preferred_element_type=jnp.float32
    )
    lane = lax.broadcasted_iota(jnp.int32, (queries, 128), 1)
    oq = jnp.where(lane < HEAD_WIDTH, out[queries:] * (1.0 / math.sqrt(HEAD_WIDTH)), out[:queries])
    oq_ref[:, pl.ds(at, TILE), :] = oq.reshape(BAND_ROWS, TILE, 128)


def attention_kernel(kv_ref, feat_ref, q_ref, g_ref, pick_ref, live_ref, oq_ref, dkv_ref):
    dkv_ref[...] = jnp.zeros_like(dkv_ref)

    @pl.loop(0, TILES)
    def _(i):
        attention_tile(i, kv_ref, feat_ref, q_ref, g_ref, pick_ref, live_ref, oq_ref, dkv_ref)

    half = TILE // 2
    oq_ref[:, :half, :] = oq_ref[:, LONGITUDES : LONGITUDES + half, :]
    dkv_ref[:, :TILE, :] += dkv_ref[:, LONGITUDES : LONGITUDES + TILE, :]


def attention(kv, feat, q, g, pick, live):
    return pl.pallas_call(
        attention_kernel,
        out_shape=(
            jax.ShapeDtypeStruct((BAND_ROWS, QUERY_COLS, 128), jnp.float32),
            jax.ShapeDtypeStruct((KEY_ROWS, KEY_COLS, 128), jnp.float32),
        ),
        in_specs=[pl.BlockSpec(memory_space=VMEM)] * 6,
        out_specs=[pl.BlockSpec(memory_space=VMEM)] * 2,
        compiler_params=pltpu.CompilerParams(vmem_limit_bytes=48 << 20),
        name="attention",
    )(kv, feat, q, g, pick, live)


def on_device(tokens, gain, qkv_weight, out_weight, row_cells, upstream):
    band_tokens = BAND_ROWS * LONGITUDES
    score_scale = 1.0 / math.sqrt(HEAD_WIDTH)
    grad_scale = 4.0 / math.sqrt(band_tokens * lax.axis_size("lat"))
    band_start = lax.axis_index("lat") * BAND_ROWS
    features = tokens.astype(jnp.float32)
    inverse = lax.rsqrt(jnp.mean(features * features, axis=1, keepdims=True) + 1e-06)
    normed = (features * inverse * gain[None, :]).astype(jnp.bfloat16)
    normed_band = lax.all_gather(normed, "mp", axis=0, tiled=True)
    cells = lax.dynamic_slice_in_dim(jnp.pad(row_cells, (REACH, REACH)), band_start, KEY_ROWS)
    qkv_flat = qkv_weight.reshape(3 * HEAD_WIDTH, WIDTH)
    qkv = lax.dot_general(
        normed_band, qkv_flat, (((1,), (1,)), ((), ())), preferred_element_type=jnp.float32
    ).astype(jnp.bfloat16)
    qkv = qkv.reshape(BAND_ROWS, LONGITUDES, 3 * HEAD_WIDTH)
    kv = qkv[..., HEAD_WIDTH:]
    before = passed_along(kv[BAND_ROWS - REACH :], "lat", 1)
    after = passed_along(kv[:REACH], "lat", -1)
    kv_all = jnp.concatenate([before, kv, after], axis=0)
    kv_all = jnp.concatenate([kv_all, kv_all[:, :TILE]], axis=1)
    out_flat = out_weight.reshape(HEAD_WIDTH, WIDTH)
    band_upstream = lax.all_gather(upstream, "mp", axis=0, tiled=True)
    grad_heads = lax.dot_general(
        band_upstream, out_flat, (((1,), (1,)), ((), ())), preferred_element_type=jnp.float32
    ).astype(jnp.bfloat16)
    half = TILE // 2
    q = jnp.pad(qkv[..., :HEAD_WIDTH].astype(jnp.float32) * score_scale, ((0, 0), (0, 0), (0, HEAD_WIDTH)))
    q = jnp.concatenate([q, q[:, :half]], axis=1)
    g = grad_heads.astype(jnp.float32).reshape(BAND_ROWS, LONGITUDES, HEAD_WIDTH)
    g = jnp.pad(g, ((0, 0), (0, 0), (HEAD_WIDTH, 0)))
    g = jnp.concatenate([g, g[:, :half]], axis=1)
    oq, dkv = attention(kv_all, key_features(cells), q, g, query_features(), live_queries(cells))
    oq = oq[:, :LONGITUDES].astype(jnp.bfloat16).reshape(band_tokens, 128)
    heads_out = oq[:, HEAD_WIDTH:]
    update = lax.psum_scatter(
        jnp.dot(heads_out, out_flat, preferred_element_type=jnp.float32).astype(jnp.bfloat16),
        "mp",
        scatter_dimension=0,
        tiled=True,
    )
    grad_out_part = lax.dot_general(
        heads_out, band_upstream, (((0,), (0,)), ((), ())), preferred_element_type=jnp.float32
    )
    dkv = dkv[:, :LONGITUDES]
    from_above = passed_along(dkv[:REACH], "lat", -1)
    from_below = passed_along(dkv[BAND_ROWS + REACH :], "lat", 1)
    own = dkv[REACH : BAND_ROWS + REACH]
    own = own.at[:REACH].add(from_below).at[BAND_ROWS - REACH :].add(from_above)
    grad_kv = own.astype(jnp.bfloat16).reshape(band_tokens, 2 * HEAD_WIDTH)
    grad_proj = jnp.concatenate([oq[:, :HEAD_WIDTH], grad_kv], axis=1)
    grad_qkv_part = lax.dot_general(
        grad_proj, normed_band, (((0,), (0,)), ((), ())), preferred_element_type=jnp.float32
    )
    grad_qkv, grad_out = lax.psum((grad_qkv_part, grad_out_part), "lat")
    grad_normed = lax.psum_scatter(
        jnp.dot(grad_proj, qkv_flat, preferred_element_type=jnp.float32).astype(jnp.bfloat16),
        "mp",
        scatter_dimension=0,
        tiled=True,
    ).astype(jnp.float32)
    centred = features * inverse
    scaled = gain[None, :] * grad_normed
    grad_input = inverse * (scaled - centred * jnp.mean(scaled * centred, axis=1, keepdims=True))
    return (
        update.astype(jnp.bfloat16),
        grad_input.astype(jnp.bfloat16),
        (grad_qkv * grad_scale).reshape(1, 3 * HEAD_WIDTH, WIDTH),
        (grad_out * grad_scale).reshape(1, HEAD_WIDTH, WIDTH),
    )


def solution(mesh):
    return jax.shard_map(
        on_device,
        mesh=mesh,
        in_specs=(
            P(("lat", "mp"), None),
            P(),
            P("mp", None, None),
            P("mp", None, None),
            P(),
            P(("lat", "mp"), None),
        ),
        out_specs=(
            P(("lat", "mp"), None),
            P(("lat", "mp"), None),
            P("mp", None, None),
            P("mp", None, None),
        ),
        check_vma=False,
    )
```

time: 853 us -> 559 us (0.66)
  local copies, waits for them, and re-layouts: 127 us -> 10.1 us
  other arithmetic: 116 us -> 14.4 us
  matrix products: 69.7 us -> 19.2 us
  loops' own time: 30.6 us -> 0 us
  Pallas kernels: 0 us -> 17.6 us
    while x16 -> x0, other arithmetic: 62.8 us -> none
    dot_general x32 -> x4, matrix products: 62.3 us -> 13.2 us  [the longest x1 4.6 us: on_device(): lax.dot_general(normed_band, qkv_flat, (((1,), (1,)), ((), ())), preferre...]
    reduce_scatter x2, waiting for transfers between devices: 224 us -> 177 us  [the longest x1 88.8 us: on_device(): lax.psum_scatter(jnp.dot(grad_proj, qkv_flat, preferred_element_type=jnp....]
    ppermute x2 -> x4, waiting for transfers between devices: 0.01 us -> 44.4 us  [passed_along(): return lax.ppermute(x, axis, pairs)]
    and x32 -> x0, local copies, waits for them, and re-layouts: 30.9 us -> none  [tile_mask(): query_live[:, :, None, None] & key_live[None, None, :, :]]
    another operation x2 -> x0, loops' own time: 30.6 us -> none  [the longest x1 20.6 us: on_device(): key_accum, query_tiles = lax.scan(backward_tile, accum_start, tile_ids)]
    another operation x19 -> x0, local copies, waits for them, and re-layouts: 26.2 us -> none  [the longest x16 23.7 us: tile_inputs(): jnp.take(lax.dynamic_slice_in_dim(keyval_ext, row_start, 16, 0), key_inde...]
    gather x8 -> x0, local copies, waits for them, and re-layouts: 22.4 us -> none  [tile_inputs(): jnp.take(lax.dynamic_slice_in_dim(keyval_ext, row_start, 16, 0), key_inde...]
  transfers between devices with their start and end apart: 9 -> 9, of which waited for: 5 -> 7; matrix products, arithmetic and copies ran while one was open for 14% -> 5% of each run, Pallas kernels for 0% -> 0%
where the time goes in v1:
time: 559 us; the launch traced here: 558 us
  waiting for transfers between devices  473 us (85%)
  matrix products  19.2 us (3%)
  Pallas kernels  17.6 us (3%)
  other arithmetic  14.4 us (3%)
  between operations  14.1 us (3%)
  local copies, waits for them, and re-layouts  10.1 us (2%)
  starting transfers between devices  9.76 us (2%)
    psum x1, waiting for transfers between devices, on_device(): grad_qkv, grad_out = lax.psum((grad_qkv_part, grad_out_part), 'lat')  136 us
    reduce_scatter x1, waiting for transfers between devices, on_device(): lax.psum_scatter(jnp.dot(grad_proj, qkv_flat, preferred_element_type=jnp....  88.8 us
    reduce_scatter x1, waiting for transfers between devices, on_device(): lax.psum_scatter(jnp.dot(heads_out, out_flat, preferred_element_type=jnp....  88.7 us
    all_gather x1, waiting for transfers between devices, on_device(): normed_band = lax.all_gather(normed, 'mp', axis=0, tiled=True)  61.3 us
    all_gather x1, waiting for transfers between devices, on_device(): band_upstream = lax.all_gather(upstream, 'mp', axis=0, tiled=True)  53.3 us
    ppermute x4, waiting for transfers between devices, passed_along(): return lax.ppermute(x, axis, pairs)  44.4 us
    pallas_call x1, Pallas kernels, attention(): pl.pallas_call(attention_kernel, out_shape=(jax.ShapeDtypeStruct((BAND_RO...  17.6 us
  transfers between devices with their start and end apart: 9, of which 7 were waited for; matrix products, arithmetic and copies ran while one was open for 5% of the time, Pallas kernels for 0%

profile of v1, /device:TPU:2, one launch (start us, length us, event | category | flops | bytes accessed | tf_op | source)
XLA Modules:
  0.0 558.2 jit_solution(15266671868716450236)
XLA Ops:
  7.2 1.1 fusion.22
  8.4 1.8 fusion.17
  10.2 0.7 all-gather.5.cloned.1.call-update
  11.0 0.7 pad_dynamic-slice_fusion
  11.7 0.1 slice.105
  11.8 0.1 iota.113
  11.9 0.1 iota.114
  12.0 0.1 lt.80
  12.1 0.1 iota.120
  12.3 0.1 compare_convert_fusion.live_ref
  12.4 0.2 fusion.35.pick_ref
  12.5 1.3 select_convert_fusion.feat_ref
  13.8 61.3 %all-gather.3.cloned.1.call-done = bf16[2048,1024]{1,0:T(8,128)(2,1)} async-done(((bf16[128,1024]{1,0:T(8,128)(2,1)}), bf16[2048,1024]{1,0:T(8,128)(2,1)}) %all-gather.3.cloned.1.call-update) | async-done | bytes 4194320 | tf_op jit(solution)/shard_map/all_gather | solution.py:143
  75.2 4.6 convolution_convert_fusion.2
  79.8 1.5 copy.10
  81.3 1.1 slice.115
  82.4 1.2 fusion.44
  83.6 1.1 convert_multiply_fusion
  84.7 53.3 %all-gather.5.cloned.1.call-done = bf16[2048,1024]{1,0:T(8,128)(2,1)} async-done(((bf16[128,1024]{1,0:T(8,128)(2,1)}), bf16[2048,1024]{1,0:T(8,128)(2,1)}) %all-gather.5.cloned.1.call-update) | async-done | bytes 4194320 | tf_op jit(solution)/shard_map/all_gather | solution.py:156
  137.9 4.3 convolution_convert_fusion.3
  142.2 1.2 copy.11
  143.5 2.5 collective-permute-start
  146.0 1.3 collective-permute-start.1
  147.3 0.2 pad_convert_fusion
  147.6 0.2 pad_maximum_fusion.2
  147.8 15.7 %collective-permute-done = bf16[6,256,128]{2,1,0:T(8,128)(2,1)S(1)} collective-permute-done((bf16[6,256,128]{2,1,0:T(8,128)(2,1)}, bf16[6,256,128]{2,1,0:T(8,128)(2,1)S(1)}, u32[]{:S(2)}, u32[]{:S(2)}) %collective-permute-start) | collective-permute-done | bytes 393248 | tf_op jit(solution)/shard_map/ppermute | solution.py:28
  163.5 0.1 fusion.11.kv_ref
  163.6 17.6 %attention.1 = (f32[8,264,128]{2,1,0:T(8,128)S(1)}, f32[20,272,128]{2,1,0:T(8,128)}) custom-call(bf16[20,272,128]{2,1,0:T(8,128)(2,1)S(1)} %fusion.11.kv_ref, bf16[20,272,128]{2,1,0:T(8,128)(2,1)S(1)} %select_convert_fusion.feat_ref, f32[8,264,128]{2,1,0:T(8,128)S(1)} %get-tuple-element.44.q_ref, f32[8,264,128]{2,1,0:T(8,128)S(1)} %get-tuple-element.45.g_ref, ...), custom_call_target="tpu_custom_call" | custom-call | tf_op jit(solution)/shard_map/attention/pallas_call | solution.py:122
  181.2 1.6 fusion.43
  182.8 4.5 collective-permute-start.2
  187.3 1.3 collective-permute-start.3
  188.6 1.3 slice.109
  190.0 1.8 fusion.23
  191.8 28.7 %collective-permute-done.2 = f32[6,256,128]{2,1,0:T(8,128)S(1)} collective-permute-done((f32[6,256,128]{2,1,0:T(8,128)S(1)}, f32[6,256,128]{2,1,0:T(8,128)S(1)}, u32[]{:S(2)}, u32[]{:S(2)}) %collective-permute-start.2) | collective-permute-done | bytes 786464 | tf_op jit(solution)/shard_map/ppermute | solution.py:28
  220.5 1.2 add_dynamic-update-slice_fusion
  221.7 0.2 fusion.12
  221.9 0.1 convert_element_type.64
  222.0 2.0 fusion.13
  224.1 3.3 convolution_convert_fusion
  227.5 0.8 copy-done.6
  228.3 3.2 convolution_convert_fusion.1
  231.6 135.8 %all-reduce.6.cloned.1.call-done = (f32[192,1024]{1,0:T(8,128)}, f32[64,1024]{1,0:T(8,128)}) async-done(((f32[192,1024]{1,0:T(8,128)}, f32[64,1024]{1,0:T(8,128)}), (f32[192,1024]{1,0:T(8,128)}, f32[64,1024]{1,0:T(8,128)})) %all-reduce.6.cloned.1.call-update) | async-done | bytes 1048592 | tf_op jit(solution)/shard_map/psum | solution.py:188
  367.4 1.7 multiply_bitcast_fusion.1
  369.1 2.1 multiply_bitcast_fusion
  371.2 88.8 %reduce-scatter.5.cloned.1.call-done = bf16[128,1024]{1,0:T(8,128)(2,1)} async-done(((bf16[2048,1024]{1,0:T(8,128)(2,1)}), bf16[128,1024]{1,0:T(8,128)(2,1)}) %reduce-scatter.5.cloned.1.call-update) | async-done | bytes 262160 | tf_op jit(solution)/shard_map/reduce_scatter | solution.py:189
  459.9 1.2 fusion.18
  461.1 1.9 fusion.21
  463.0 88.7 %reduce-scatter.3.cloned.1.call-done = bf16[128,1024]{1,0:T(8,128)(2,1)} async-done(((bf16[2048,1024]{1,0:T(8,128)(2,1)}), bf16[128,1024]{1,0:T(8,128)(2,1)}) %reduce-scatter.3.cloned.1.call-update) | async-done | bytes 262160 | tf_op jit(solution)/shard_map/reduce_scatter | solution.py:169
  (44 shorter events, 0.6 us)
Async XLA Ops:
  7.2 68.0 %copy-start = (bf16[1,192,1024]{2,1,0:T(8,128)(2,1)S(1)}, bf16[1,192,1024]{2,1,0:T(8,128)(2,1)}, u32[]{:S(2)}) copy-start(bf16[1,192,1024]{2,1,0:T(8,128)(2,1)} %param.12) | copy-start | bytes 1179652
  7.2 68.0 %all-gather.3.cloned.1.call-start = ((), (), s32[]{:S(2)}) async-start(), calls=%async_computation.2 | async-start | bytes 4456448 | tf_op jit(solution)/shard_map/all_gather | solution.py:143
  10.2 127.8 %all-gather.5.cloned.1.call-start = ((), (), s32[]{:S(2)}) async-start(), calls=%async_computation.3 | async-start | bytes 4456448 | tf_op jit(solution)/shard_map/all_gather | solution.py:156
  10.9 356.5 %all-reduce.6.cloned.1.call-start = ((), (), s32[]{:S(2)}) async-start(), calls=%async_computation.6 | async-start | bytes 2097152 | tf_op jit(solution)/shard_map/psum | solution.py:188
  79.8 58.2 %copy-start.5 = (bf16[1,64,1024]{2,1,0:T(8,128)(2,1)S(1)}, bf16[1,64,1024]{2,1,0:T(8,128)(2,1)}, u32[]{:S(2)}) copy-start(bf16[1,64,1024]{2,1,0:T(8,128)(2,1)} %param.13) | copy-start | bytes 393220
  81.3 1.1 copy-start.2
  143.5 20.0 %collective-permute-start = (bf16[6,256,128]{2,1,0:T(8,128)(2,1)}, bf16[6,256,128]{2,1,0:T(8,128)(2,1)S(1)}, u32[]{:S(2)}, u32[]{:S(2)}) collective-permute-start(bf16[6,256,128]{2,1,0:T(8,128)(2,1)} %get-tuple-element.36), channel_id=1, source_target_pairs={{0,16},{16,32},{32,48},{48,64},{64,80},{80,96},{96,112},{112,128},... | collective-permute-start | bytes 1179656 | tf_op jit(solution)/shard_map/ppermute | solution.py:28
  146.0 17.5 %collective-permute-start.1 = (bf16[6,256,128]{2,1,0:T(8,128)(2,1)}, bf16[6,256,128]{2,1,0:T(8,128)(2,1)S(1)}, u32[]{:S(2)}, u32[]{:S(2)}) collective-permute-start(bf16[6,256,128]{2,1,0:T(8,128)(2,1)} %get-tuple-element.37), channel_id=1, source_target_pairs={{16,0},{32,16},{48,32},{64,48},{80,64},{96,80},{112,96},{128,112},... | collective-permute-start | bytes 1179656 | tf_op jit(solution)/shard_map/ppermute | solution.py:28
  147.6 15.9 %copy-start.4 = (bf16[8,256,128]{2,1,0:T(8,128)(2,1)S(1)}, bf16[8,256,128]{2,1,0:T(8,128)(2,1)}, u32[]{:S(2)}) copy-start(bf16[8,256,128]{2,1,0:T(8,128)(2,1)} %slice.115) | copy-start | bytes 1572868
  181.2 8.8 %copy-start.1 = (bf16[2048,1024]{1,0:T(8,128)(2,1)S(1)}, bf16[2048,1024]{1,0:T(8,128)(2,1)}, u32[]{:S(2)}) copy-start(bf16[2048,1024]{1,0:T(8,128)(2,1)} %all-gather.5.cloned.1.call-done) | copy-start | bytes 12582916
  182.8 37.7 %collective-permute-start.2 = (f32[6,256,128]{2,1,0:T(8,128)S(1)}, f32[6,256,128]{2,1,0:T(8,128)S(1)}, u32[]{:S(2)}, u32[]{:S(2)}) collective-permute-start(f32[6,256,128]{2,1,0:T(8,128)S(1)} %get-tuple-element.35), channel_id=1, source_target_pairs={{0,16},{16,32},{32,48},{48,64},{64,80},{80,96},{96,112},{112,128},... | collective-permute-start | bytes 2359304 | tf_op jit(solution)/shard_map/ppermute | solution.py:28
  187.3 34.4 %collective-permute-start.3 = (f32[6,256,128]{2,1,0:T(8,128)S(1)}, f32[6,256,128]{2,1,0:T(8,128)S(1)}, u32[]{:S(2)}, u32[]{:S(2)}) collective-permute-start(f32[6,256,128]{2,1,0:T(8,128)S(1)} %get-tuple-element.34), channel_id=1, source_target_pairs={{16,0},{32,16},{48,32},{64,48},{80,64},{96,80},{112,96},{128,112},... | collective-permute-start | bytes 2359304 | tf_op jit(solution)/shard_map/ppermute | solution.py:28
  191.8 30.2 %copy-start.8 = (bf16[2048,1024]{1,0:T(8,128)(2,1)S(1)}, bf16[2048,1024]{1,0:T(8,128)(2,1)}, u32[]{:S(2)}) copy-start(bf16[2048,1024]{1,0:T(8,128)(2,1)} %all-gather.3.cloned.1.call-done) | copy-start | bytes 12582916
  224.0 235.9 %reduce-scatter.5.cloned.1.call-start = ((), (), s32[]{:S(2)}) async-start(), calls=%async_computation.5 | async-start | bytes 4456448 | tf_op jit(solution)/shard_map/reduce_scatter | solution.py:189
  227.4 0.9 copy-start.6
  227.4 324.3 %reduce-scatter.3.cloned.1.call-start = ((), (), s32[]{:S(2)}) async-start(), calls=%async_computation.4 | async-start | bytes 4456448 | tf_op jit(solution)/shard_map/reduce_scatter | solution.py:169
  231.5 228.4 %copy-start.3 = (bf16[128,1024]{1,0:T(8,128)(2,1)S(1)}, bf16[128,1024]{1,0:T(8,128)(2,1)}, u32[]{:S(2)}) copy-start(bf16[128,1024]{1,0:T(8,128)(2,1)} %param.10) | copy-start | bytes 786436
  231.5 228.4 %copy-start.7 = (f32[1024]{0:T(1024)S(1)}, f32[1024]{0:T(1024)}, u32[]{:S(2)}) copy-start(f32[1024]{0:T(1024)} %param.11) | copy-start | bytes 12292
Sparse Core Ops, SparseCore 0:
  11.3 63.8 all-gather.2
  77.9 59.9 all-gather.4
  224.2 143.1 all-reduce.5
  372.2 87.6 reduce-scatter.4
  464.7 86.9 reduce-scatter.2

commit v2 on v1

v2 whole, which is shorter than its diff:
```python
import math

import jax
import jax.numpy as jnp
from jax import lax
from jax.experimental import pallas as pl
from jax.experimental.pallas import tpu as pltpu
from jax.sharding import PartitionSpec as P

WIDTH = 1024
HEAD_WIDTH = 64
LONGITUDES = 256
BAND_ROWS = 8
REACH = 6
KEY_ROWS = BAND_ROWS + 2 * REACH
TILE = 16
WINDOW = 2 * TILE
TILES = LONGITUDES // TILE
KEY_COLS = LONGITUDES + TILE
QUERY_COLS = LONGITUDES + TILE // 2
NEVER = -1e30
VMEM = pltpu.VMEM
MESH = pl.DeviceIdType.MESH
HALF = LONGITUDES // 2
BF = jnp.bfloat16
F32 = jnp.float32
DMA = pltpu.SemaphoreType.DMA


def key_features(cells):
    shape = (KEY_ROWS, KEY_COLS, 128)
    row = lax.broadcasted_iota(jnp.int32, shape, 0)
    col = lax.broadcasted_iota(jnp.int32, shape, 1)
    lane = lax.broadcasted_iota(jnp.int32, shape, 2)
    live = col % LONGITUDES < cells[:, None, None]
    near_row = (row >= lane - 8) & (row <= lane - 8 + 2 * REACH)
    apart = (col - lane) % 32
    near_col = (apart <= REACH) | (apart >= 32 - REACH)
    barred = (
        ((lane == 0) & ~live)
        | ((lane >= 8) & (lane < 16) & ~near_row)
        | ((lane >= 32) & (lane < 64) & ~near_col)
    )
    return jnp.where(barred, NEVER, 0.0).astype(jnp.bfloat16)


def query_features():
    shape = (2, BAND_ROWS, TILE, 128)
    tile, row, col, lane = (lax.broadcasted_iota(jnp.int32, shape, d) for d in range(4))
    picked = (
        (lane == 0)
        | (lane == 8 + row)
        | (lane == 32 + (TILE * tile + TILE // 2 + col) % 32)
    )
    return picked.astype(jnp.bfloat16).reshape(2, BAND_ROWS * TILE, 128)


def live_queries(cells):
    shape = (TILES, 1, BAND_ROWS, TILE)
    tile, _, _, col = (lax.broadcasted_iota(jnp.int32, shape, d) for d in range(4))
    at = (TILE * tile + TILE // 2 + col) % LONGITUDES
    live = at < cells[REACH : REACH + BAND_ROWS][None, None, :, None]
    return live.astype(jnp.float32).reshape(TILES, 1, BAND_ROWS * TILE)


def attention_tile(i, kv_ref, feat_ref, q_ref, g_ref, pick_ref, live_ref, oq_ref, dkv_ref):
    queries = BAND_ROWS * TILE
    keys = KEY_ROWS * WINDOW
    c0 = pl.multiple_of(i * TILE, TILE)
    at = pl.multiple_of(i * TILE + TILE // 2, TILE // 2)
    kv = kv_ref[:, pl.ds(c0, WINDOW), :].reshape(keys, 128)
    feat = feat_ref[:, pl.ds(c0, WINDOW), :].reshape(keys, 128)
    q = q_ref[:, pl.ds(at, TILE), :].reshape(queries, 128).astype(jnp.bfloat16)
    g = g_ref[:, pl.ds(at, TILE), :].reshape(queries, 128).astype(jnp.bfloat16)
    pick = pick_ref[lax.rem(i, 2)]
    both = jnp.concatenate(
        [
            jnp.concatenate([q, pick], axis=1),
            jnp.concatenate([g, jnp.zeros_like(g)], axis=1),
        ],
        axis=0,
    )
    products = lax.dot_general(
        jnp.concatenate([kv, feat], axis=1),
        both,
        (((1,), (1,)), ((), ())),
        preferred_element_type=jnp.float32,
    )
    scores = products[:, :queries]
    grad_probs = products[:, queries:]
    highest = jnp.max(scores, axis=0, keepdims=True)
    terms = jnp.exp(scores - highest)
    probs = terms * (live_ref[i] / jnp.sum(terms, axis=0, keepdims=True))
    weights = probs.astype(jnp.bfloat16)
    row_delta = jnp.sum(probs * grad_probs, axis=0, keepdims=True)
    grad_scores = (probs * (grad_probs - row_delta)).astype(jnp.bfloat16)
    pair = jnp.concatenate([weights, grad_scores], axis=1)
    dkv = jnp.dot(pair, jnp.concatenate([g, q], axis=0), preferred_element_type=jnp.float32)
    dkv_ref[:, pl.ds(c0, WINDOW), :] += dkv.reshape(KEY_ROWS, WINDOW, 128)
    out = lax.dot_general(
        pair, kv, (((0,), (0,)), ((), ())), preferred_element_type=jnp.float32
    )
    lane = lax.broadcasted_iota(jnp.int32, (queries, 128), 1)
    oq = jnp.where(lane < HEAD_WIDTH, out[queries:] * (1.0 / math.sqrt(HEAD_WIDTH)), out[:queries])
    oq_ref[:, pl.ds(at, TILE), :] = oq.reshape(BAND_ROWS, TILE, 128)


def remote(src, dst, send_sem, recv_sem, device):
    return pltpu.make_async_remote_copy(
        src_ref=src,
        dst_ref=dst,
        send_sem=send_sem,
        recv_sem=recv_sem,
        device_id=device,
        device_id_type=MESH,
    )


def sublayer_kernel(
    tok_ref, gain_ref, w_ref, wo_ref, up_ref, feat_ref, pick_ref, live_ref,
    update_ref, grad_in_ref, grad_qkv_ref, grad_out_ref,
    nb, ub, wp, wo, kv, q, g, oq, dkv, hs, hr, ab, asib, us, ur, gs, gr, mine, wg, wgb, lr, lf,
    sn, rn, snf, rnf, su, ru, suf, ruf, sw, rw, sh, rh, shg, rhg, sa, ra, sup, rup, sgn, rgn, sl, rl, sf, rf,
):
    lat, mp = lax.axis_index("lat"), lax.axis_index("mp")
    y, x, core = mp // 8, (mp // 2) % 4, mp % 2
    me = mp // 2
    sibling = {"mp": me * 2 + (1 - core)}
    own_half = pl.ds(pl.multiple_of(core * HALF, HALF), HALF)
    other_half = pl.ds(pl.multiple_of((1 - core) * HALF, HALF), HALF)

    def chip(k):
        d = k % 4
        d = d + (d // 2) * (1 - 2 * (d % 2))
        return ((y + k // 4) % 2) * 4 + (x + d) % 4

    def peer(row):
        return {"mp": row * 2 + core}

    def along(step):
        return {"lat": (lat + step) % 16}

    barrier = pltpu.get_barrier_semaphore()

    @pl.loop(1, 8)
    def _(k):
        pl.semaphore_signal(barrier, inc=1, device_id=peer(chip(k)), device_id_type=MESH)

    pl.semaphore_signal(barrier, inc=1, device_id=sibling, device_id_type=MESH)

    @pl.loop(1, 16)
    def _(k):
        pl.semaphore_signal(barrier, inc=1, device_id=along(k), device_id_type=MESH)

    def normalised():
        features = tok_ref[...].astype(F32)
        inverse = lax.rsqrt(jnp.mean(features * features, axis=1, keepdims=True) + 1e-06)
        return features, inverse

    features, inverse = normalised()
    nb[me, own_half, :] = (features * inverse * gain_ref[...]).astype(BF)
    ub[me, own_half, :] = up_ref[...]
    wp[0:64, :] = w_ref[0:64, :]
    wp[64:128, :] = jnp.zeros((64, WIDTH), BF)
    wp[128:256, :] = w_ref[64:192, :]
    wo[0:64, :] = jnp.zeros((64, WIDTH), BF)
    wo[64:128, :] = wo_ref[...]
    pl.semaphore_wait(barrier, 23)

    def spread(buf, s, r, k):
        return remote(buf.at[me, own_half], buf.at[me, own_half], s.at[k], r.at[me], peer(chip(k)))

    def arrived(buf, s, r, row):
        return remote(buf.at[row, own_half], buf.at[row, own_half], s.at[0], r.at[row], peer(row))

    def handed(buf, s, r, row):
        return remote(buf.at[row, own_half], buf.at[row, own_half], s.at[row], r.at[row], sibling)

    def handed_in(buf, s, r, row):
        return remote(buf.at[row, other_half], buf.at[row, other_half], s.at[row], r.at[row], sibling)

    @pl.loop(1, 8)
    def _(k):
        spread(nb, sn, rn, k).start()

    handed(nb, snf, rnf, me).start()
    handed(ub, suf, ruf, me).start()
    weights_over = remote(wp.at[0:256], wp.at[256:512], sw.at[0], rw.at[0], sibling)
    weights_over.start()
    out_weights_over = remote(wo.at[0:128], wo.at[128:256], sw.at[1], rw.at[1], sibling)
    out_weights_over.start()
    dkv[...] = jnp.zeros_like(dkv)

    def project(row):
        handed_in(nb, snf, rnf, row).wait_recv()
        made = lax.dot_general(
            nb[row], wp[0:256, :], (((1,), (1,)), ((), ())), preferred_element_type=F32
        ).astype(BF)
        scaled = made[:, 0:128].astype(F32) * (1.0 / math.sqrt(HEAD_WIDTH))
        q[row, 0:LONGITUDES, :] = scaled
        q[row, LONGITUDES:QUERY_COLS, :] = scaled[0 : TILE // 2]
        kv[REACH + row, 0:LONGITUDES, :] = made[:, 128:256]
        kv[REACH + row, LONGITUDES:KEY_COLS, :] = made[0:TILE, 128:256]

    def project_upstream(row):
        handed_in(ub, suf, ruf, row).wait_recv()
        made = lax.dot_general(
            ub[row], wo[0:128, :], (((1,), (1,)), ((), ())), preferred_element_type=F32
        ).astype(BF)
        made = made.astype(F32)
        g[row, 0:LONGITUDES, :] = made
        g[row, LONGITUDES:QUERY_COLS, :] = made[0 : TILE // 2]

    @pl.loop(1, 8)
    def _(k):
        row = chip(k)
        arrived(nb, sn, rn, row).wait_recv()
        handed(nb, snf, rnf, row).start()
        project(chip(k - 1))
        spread(nb, sn, rn, k).wait_send()
        spread(ub, su, ru, k).start()

    project(chip(7))

    up_halo = remote(kv.at[BAND_ROWS : BAND_ROWS + REACH], kv.at[0:REACH], sh.at[0], rh.at[0], along(1))
    up_halo.start()
    down_halo = remote(kv.at[REACH : 2 * REACH], kv.at[BAND_ROWS + REACH : KEY_ROWS], sh.at[1], rh.at[1], along(15))
    down_halo.start()

    @pl.loop(1, 8)
    def _(k):
        row = chip(k)
        arrived(ub, su, ru, row).wait_recv()
        handed(ub, suf, ruf, row).start()
        project_upstream(chip(k - 1))

    project_upstream(chip(7))
    up_halo.wait()
    down_halo.wait()

    @pl.loop(0, TILES)
    def _(i):
        attention_tile(i, kv, feat_ref, q, g, pick_ref, live_ref, oq, dkv)

    half = TILE // 2
    oq[:, :half, :] = oq[:, LONGITUDES : LONGITUDES + half, :]
    dkv[:, :TILE, :] += dkv[:, LONGITUDES : LONGITUDES + TILE, :]
    hs[0] = dkv[0:REACH, 0:LONGITUDES, :].astype(BF)
    hs[1] = dkv[BAND_ROWS + REACH : KEY_ROWS, 0:LONGITUDES, :].astype(BF)
    down_grad = remote(hs.at[0], hr.at[0], shg.at[0], rhg.at[0], along(15))
    down_grad.start()
    up_grad = remote(hs.at[1], hr.at[1], shg.at[1], rhg.at[1], along(1))
    up_grad.start()
    ab[:, :, 0:128] = oq[:, 0:LONGITUDES, :].astype(BF)
    oq_over = remote(ab.at[:, other_half, 0:128], asib.at[:, :, 0:128], sa.at[0], ra.at[0], sibling)
    oq_over.start()

    columns = 512

    @pl.loop(0, WIDTH // columns)
    def _(n):
        cut = pl.ds(pl.multiple_of(n * columns, columns), columns)
        part = lax.dot_general(
            ab[:, :, 0:128].reshape(BAND_ROWS * LONGITUDES, 128),
            ub[:, :, cut].reshape(BAND_ROWS * LONGITUDES, columns),
            (((0,), (0,)), ((), ())),
            preferred_element_type=F32,
        )
        wg[192:256, cut] = part[64:128]

    out_weights_over.wait()
    oq_over.wait()

    def sent(buf, into, s, r, k):
        row = chip(k)
        return remote(buf.at[row], into.at[me], s.at[k], r.at[me], peer(row))

    def received(into, s, r, row):
        return remote(into.at[row], into.at[row], s.at[0], r.at[row], peer(row))

    def update_part(row):
        both = jnp.concatenate([ab[row, own_half, 0:128], asib[row, :, 0:128]], axis=1)
        return jnp.dot(both, wo[...], preferred_element_type=F32)

    @pl.loop(1, 8)
    def _(k):
        us[chip(k)] = update_part(chip(k)).astype(BF)
        sent(us, ur, sup, rup, k).start()

    mine[0] = update_part(me)
    down_grad.wait()
    up_grad.wait()
    dkv[BAND_ROWS : BAND_ROWS + REACH, 0:LONGITUDES, :] += hr[0].astype(F32)
    dkv[REACH : 2 * REACH, 0:LONGITUDES, :] += hr[1].astype(F32)
    ab[:, :, 128:256] = dkv[REACH : REACH + BAND_ROWS, 0:LONGITUDES, :].astype(BF)
    kv_over = remote(ab.at[:, other_half, 128:256], asib.at[:, :, 128:256], sa.at[1], ra.at[1], sibling)
    kv_over.start()
    weights_over.wait()
    kv_over.wait()

    def grad_part(row):
        both = jnp.concatenate([ab[row, own_half, :], asib[row]], axis=1)
        return jnp.dot(both, wp[...], preferred_element_type=F32)

    @pl.loop(1, 8)
    def _(k):
        gs[chip(k)] = grad_part(chip(k)).astype(BF)
        sent(gs, gr, sgn, rgn, k).start()

    mine[1] = grad_part(me)

    @pl.loop(0, WIDTH // columns)
    def _(n):
        cut = pl.ds(pl.multiple_of(n * columns, columns), columns)
        part = lax.dot_general(
            ab[...].reshape(BAND_ROWS * LONGITUDES, 256),
            nb[:, :, cut].reshape(BAND_ROWS * LONGITUDES, columns),
            (((0,), (0,)), ((), ())),
            preferred_element_type=F32,
        )
        wg[0:64, cut] = part[0:64]
        wg[64:192, cut] = part[128:256]

    wgb[...] = wg[...].astype(BF)

    def share(row):
        return pl.ds(pl.multiple_of(row * 16, 16), 16)

    def scatter(k):
        to = (lat + k) % 16
        return remote(wgb.at[share(to)], lr.at[k], sl.at[k], rl.at[k], along(k))

    def gather(k):
        return remote(lf.at[share(lat)], lf.at[share(lat)], sf.at[k], rf.at[k], along(k))

    def gathered(k):
        row = (lat + 16 - k) % 16
        return remote(lf.at[share(row)], lf.at[share(row)], sf.at[k], rf.at[k], along(k))

    @pl.loop(1, 16)
    def _(k):
        scatter(k).start()

    lr[0] = wgb[share(lat), :]
    total = wg[share(lat), :]
    for k in range(1, 16):
        scatter(k).wait()
        total = total + lr[k].astype(F32)
    lf[share(lat), :] = (total * (4.0 / math.sqrt(BAND_ROWS * LONGITUDES * 16))).astype(BF)

    @pl.loop(1, 16)
    def _(k):
        gather(k).start()

    total = mine[0]
    for k in range(1, 8):
        received(ur, sup, rup, chip(k)).wait_recv()
        total = total + ur[chip(k)].astype(F32)
    update_ref[...] = total.astype(BF)

    total = mine[1]
    for k in range(1, 8):
        received(gr, sgn, rgn, chip(k)).wait_recv()
        total = total + gr[chip(k)].astype(F32)
    features, inverse = normalised()
    centred = features * inverse
    scaled = gain_ref[...] * total
    grad_in_ref[...] = (
        inverse * (scaled - centred * jnp.mean(scaled * centred, axis=1, keepdims=True))
    ).astype(BF)

    @pl.loop(1, 16)
    def _(k):
        gather(k).wait_send()
        gathered(k).wait_recv()

    grad_qkv_ref[...] = lf[0:192, :].astype(F32)
    grad_out_ref[...] = lf[192:256, :].astype(F32)

    @pl.loop(1, 8)
    def _(k):
        spread(ub, su, ru, k).wait_send()
        sent(us, ur, sup, rup, k).wait_send()
        sent(gs, gr, sgn, rgn, k).wait_send()

    @pl.loop(0, 8)
    def _(k):
        handed(nb, snf, rnf, k).wait_send()
        handed(ub, suf, ruf, k).wait_send()


def on_device(tokens, gain, qkv_weight, out_weight, row_cells, upstream):
    band_start = lax.axis_index("lat") * BAND_ROWS
    cells = lax.dynamic_slice_in_dim(jnp.pad(row_cells, (REACH, REACH)), band_start, KEY_ROWS)
    shape = (BAND_ROWS, LONGITUDES, WIDTH)
    queries = (BAND_ROWS, QUERY_COLS, 128)
    keys = (KEY_ROWS, KEY_COLS, 128)
    halo = (2, REACH, LONGITUDES, 128)
    blocks = (8, HALF, WIDTH)
    update, grad_input, grad_qkv, grad_out = pl.pallas_call(
        sublayer_kernel,
        out_shape=(
            jax.ShapeDtypeStruct((HALF, WIDTH), BF),
            jax.ShapeDtypeStruct((HALF, WIDTH), BF),
            jax.ShapeDtypeStruct((3 * HEAD_WIDTH, WIDTH), F32),
            jax.ShapeDtypeStruct((HEAD_WIDTH, WIDTH), F32),
        ),
        in_specs=[pl.BlockSpec(memory_space=VMEM)] * 8,
        out_specs=[pl.BlockSpec(memory_space=VMEM)] * 4,
        scratch_shapes=[
            VMEM(shape, BF),
            VMEM(shape, BF),
            VMEM((512, WIDTH), BF),
            VMEM((256, WIDTH), BF),
            VMEM(keys, BF),
            VMEM(queries, F32),
            VMEM(queries, F32),
            VMEM(queries, F32),
            VMEM(keys, F32),
            VMEM(halo, BF),
            VMEM(halo, BF),
            VMEM((BAND_ROWS, LONGITUDES, 256), BF),
            VMEM((BAND_ROWS, HALF, 256), BF),
            VMEM(blocks, BF),
            VMEM(blocks, BF),
            VMEM(blocks, BF),
            VMEM(blocks, BF),
            VMEM((2, HALF, WIDTH), F32),
            VMEM((256, WIDTH), F32),
            VMEM((256, WIDTH), BF),
            VMEM((16, 16, WIDTH), BF),
            VMEM((256, WIDTH), BF),
        ]
        + [DMA((8,))] * 8
        + [DMA((2,))] * 8
        + [DMA((8,))] * 4
        + [DMA((16,))] * 4,
        compiler_params=pltpu.CompilerParams(
            collective_id=0, has_side_effects=True, vmem_limit_bytes=56 << 20
        ),
        name="sublayer",
    )(
        tokens,
        gain.reshape(1, WIDTH),
        qkv_weight.reshape(3 * HEAD_WIDTH, WIDTH),
        out_weight.reshape(HEAD_WIDTH, WIDTH),
        upstream,
        key_features(cells),
        query_features(),
        live_queries(cells),
    )
    return (
        update,
        grad_input,
        grad_qkv.reshape(1, 3 * HEAD_WIDTH, WIDTH),
        grad_out.reshape(1, HEAD_WIDTH, WIDTH),
    )


def solution(mesh):
    return jax.shard_map(
        on_device,
        mesh=mesh,
        in_specs=(
            P(("lat", "mp"), None),
            P(),
            P("mp", None, None),
            P("mp", None, None),
            P(),
            P(("lat", "mp"), None),
        ),
        out_specs=(
            P(("lat", "mp"), None),
            P(("lat", "mp"), None),
            P("mp", None, None),
            P("mp", None, None),
        ),
        check_vma=False,
    )
```

time: 559 us -> 194 us (0.35)
  the two profiles are of different devices: /device:TPU:2 before, /device:TPU:28 now
where the time goes in v2:
time: 194 us
  Pallas kernels  184 us (95%)
  local copies, waits for them, and re-layouts  6.21 us (3%)
  other arithmetic  3.64 us (2%)
    pallas_call x1, Pallas kernels, on_device(): pl.pallas_call(sublayer_kernel, out_shape=(jax.ShapeDtypeStruct((HALF, WI...  184 us
    unnamed x8, local copies, waits for them, and re-layouts  5.01 us

profile of v2, /device:TPU:28, one launch (start us, length us, event | category | flops | bytes accessed | tf_op | source)
XLA Modules:
  0.0 194.1 jit_solution(7683684657740697778)
XLA Ops:
  0.6 0.7 pad_dynamic-slice_fusion
  1.4 0.1 slice.3
  1.5 0.1 iota.113
  1.6 0.1 iota.114
  1.6 0.1 lt.79
  1.7 0.1 lt.80
  1.8 0.1 iota.120
  1.9 0.7 compare_convert_fusion.live_ref
  2.6 0.8 fusion.16.pick_ref
  3.4 2.1 %select_convert_fusion.feat_ref = bf16[20,272,128]{2,1,0:T(8,128)(2,1)} fusion(s32[128]{0:T(128)S(1)} %get-tuple-element.17, s32[128]{0:T(128)S(1)} %get-tuple-element.16, s32[20]{0:T(128)S(1)} %pad_dynamic-slice_fusion, s32[272]{0:T(512)S(1)} %get-tuple-element.12, s32[272]{0:T(512)S(1)} %get-tuple-element.13, pred[272]{0:T(512)(128)(4,1)S(1)} %fusion.21, ...), kind=kLoop, calls=%fused_computation.6 | loop fusion | flops 20889600 | bytes 1396576 | tf_op jit(solution)/shard_map/convert_element_type | solution.py:44
  5.5 183.5 %sublayer.1 = (bf16[128,1024]{1,0:T(8,128)(2,1)}, bf16[128,1024]{1,0:T(8,128)(2,1)}, f32[192,1024]{1,0:T(8,128)}, f32[64,1024]{1,0:T(8,128)}) custom-call(bf16[128,1024]{1,0:T(8,128)(2,1)} %tok_ref.1, f32[1,1024]{1,0:T(1,128)} %bitcast.9, bf16[192,1024]{1,0:T(8,128)(2,1)} %bitcast.6, bf16[64,1024]{1,0:T(8,128)(2,1)} %bitcast.8, bf16[128,1024]{1,0:T(8,128)(2,1)} %up_ref.1, ...), custom_call_target="tpu_custom_call" | custom-call | tf_op jit(solution)/shard_map/sublayer/pallas_call | solution.py:400
  189.0 0.0 copy-start
  189.1 0.0 copy-start.1
  189.1 1.8 copy.14
  190.8 1.7 copy.15
  192.5 0.0 copy-done
  192.5 0.9 copy.16
  193.4 0.0 copy-done.1
  193.4 0.7 copy.17
  (9 shorter events, 0.0 us)
Async XLA Ops:
  189.0 3.4 %copy-start = (f32[192,1024]{1,0:T(8,128)S(1)}, f32[192,1024]{1,0:T(8,128)}, u32[]{:S(2)}) copy-start(f32[192,1024]{1,0:T(8,128)} %get-tuple-element.10) | copy-start | bytes 2359300
  189.1 4.3 %copy-start.1 = (f32[64,1024]{1,0:T(8,128)S(1)}, f32[64,1024]{1,0:T(8,128)}, u32[]{:S(2)}) copy-start(f32[64,1024]{1,0:T(8,128)} %get-tuple-element.11) | copy-start | bytes 786436

commit v3 on v2

--- a/solution.py
+++ b/solution.py
@@ -119,15 +119,24 @@
 def sublayer_kernel(
     tok_ref, gain_ref, w_ref, wo_ref, up_ref, feat_ref, pick_ref, live_ref,
     update_ref, grad_in_ref, grad_qkv_ref, grad_out_ref,
-    nb, ub, wp, wo, kv, q, g, oq, dkv, hs, hr, ab, asib, us, ur, gs, gr, mine, wg, wgb, lr, lf,
-    sn, rn, snf, rnf, su, ru, suf, ruf, sw, rw, sh, rh, shg, rhg, sa, ra, sup, rup, sgn, rgn, sl, rl, sf, rf,
+    nb, ub, wp, wall, kv, q, g, oq, dkv, hs, hr, ab, asib, ds, gb, os, oa, gs, gr, gy, mine, wg, wgb, wx, lr, lf,
+    sn, rn, snf, rnf, su, ru, sw, rw, swf, rwf, sku, rku, skd, rkd, shg, rhg, so, ro, sgn, rgn,
+    sd, rd, sl, rl, sf, rf, sp, rp,
 ):
     lat, mp = lax.axis_index("lat"), lax.axis_index("mp")
     y, x, core = mp // 8, (mp // 2) % 4, mp % 2
     me = mp // 2
+    across = (1 - y) * 4 + x
     sibling = {"mp": me * 2 + (1 - core)}
-    own_half = pl.ds(pl.multiple_of(core * HALF, HALF), HALF)
-    other_half = pl.ds(pl.multiple_of((1 - core) * HALF, HALF), HALF)
+
+    def halves(width):
+        return (
+            pl.ds(pl.multiple_of(core * width, width), width),
+            pl.ds(pl.multiple_of((1 - core) * width, width), width),
+        )
+
+    own_half, other_half = halves(HALF)
+    own_head, other_head = halves(HEAD_WIDTH)
 
     def chip(k):
         d = k % 4
@@ -142,14 +151,9 @@
 
     barrier = pltpu.get_barrier_semaphore()
 
-    @pl.loop(1, 8)
-    def _(k):
-        pl.semaphore_signal(barrier, inc=1, device_id=peer(chip(k)), device_id_type=MESH)
-
-    pl.semaphore_signal(barrier, inc=1, device_id=sibling, device_id_type=MESH)
-
     @pl.loop(1, 16)
     def _(k):
+        pl.semaphore_signal(barrier, inc=1, device_id={"mp": (mp + k) % 16}, device_id_type=MESH)
         pl.semaphore_signal(barrier, inc=1, device_id=along(k), device_id_type=MESH)
 
     def normalised():
@@ -159,101 +163,280 @@
 
     features, inverse = normalised()
     nb[me, own_half, :] = (features * inverse * gain_ref[...]).astype(BF)
-    ub[me, own_half, :] = up_ref[...]
+    ub[me] = up_ref[...]
+    wall[me, own_head, :] = wo_ref[...]
     wp[0:64, :] = w_ref[0:64, :]
     wp[64:128, :] = jnp.zeros((64, WIDTH), BF)
     wp[128:256, :] = w_ref[64:192, :]
-    wo[0:64, :] = jnp.zeros((64, WIDTH), BF)
-    wo[64:128, :] = wo_ref[...]
-    pl.semaphore_wait(barrier, 23)
-
-    def spread(buf, s, r, k):
-        return remote(buf.at[me, own_half], buf.at[me, own_half], s.at[k], r.at[me], peer(chip(k)))
-
-    def arrived(buf, s, r, row):
-        return remote(buf.at[row, own_half], buf.at[row, own_half], s.at[0], r.at[row], peer(row))
-
-    def handed(buf, s, r, row):
-        return remote(buf.at[row, own_half], buf.at[row, own_half], s.at[row], r.at[row], sibling)
-
-    def handed_in(buf, s, r, row):
-        return remote(buf.at[row, other_half], buf.at[row, other_half], s.at[row], r.at[row], sibling)
-
-    @pl.loop(1, 8)
-    def _(k):
-        spread(nb, sn, rn, k).start()
-
-    handed(nb, snf, rnf, me).start()
-    handed(ub, suf, ruf, me).start()
-    weights_over = remote(wp.at[0:256], wp.at[256:512], sw.at[0], rw.at[0], sibling)
+    pl.semaphore_wait(barrier, 30)
+
+    def blocks(buf, cut, s, r):
+        def at(row):
+            return buf.at[row] if cut is None else buf.at[row, cut]
+
+        def own(k):
+            return remote(at(me), at(me), s.at[k], r.at[me], peer(chip(k)))
+
+        def passed(k):
+            return remote(at(across), at(across), s.at[k + 4], r.at[across], peer(chip(k)))
+
+        def arrived(row):
+            return remote(at(row), at(row), s.at[0], r.at[row], peer(row))
+
+        return own, passed, arrived
+
+    def handing(buf, cut, cut_in, s, r):
+        def out(row):
+            return remote(buf.at[row, cut], buf.at[row, cut], s.at[row], r.at[row], sibling)
+
+        def into(row):
+            return remote(buf.at[row, cut_in], buf.at[row, cut_in], s.at[row], r.at[row], sibling)
+
+        return out, into
+
+    n_own, n_passed, n_arrived = blocks(nb, own_half, sn, rn)
+    n_out, n_in = handing(nb, own_half, other_half, snf, rnf)
+    w_own, w_passed, w_arrived = blocks(wall, own_head, sw, rw)
+    w_out, w_in = handing(wall, own_head, other_head, swf, rwf)
+    u_own, u_passed, u_arrived = blocks(ub, None, su, ru)
+
+    n_own(4).start()
+
+    @pl.loop(1, 4)
+    def _(k):
+        n_own(k).start()
+
+    n_out(me).start()
+    w_out(me).start()
+    weights_over = remote(wp.at[0:256], wp.at[256:512], sp.at[0], rp.at[0], sibling)
     weights_over.start()
-    out_weights_over = remote(wo.at[0:128], wo.at[128:256], sw.at[1], rw.at[1], sibling)
-    out_weights_over.start()
     dkv[...] = jnp.zeros_like(dkv)
 
+    def up_halo(row):
+        return remote(kv.at[REACH + row], kv.at[row + REACH - BAND_ROWS], sku.at[row], rku.at[row], along(1))
+
+    def down_halo(row):
+        return remote(kv.at[REACH + row], kv.at[row + REACH + BAND_ROWS], skd.at[row], rkd.at[row], along(15))
+
     def project(row):
-        handed_in(nb, snf, rnf, row).wait_recv()
+        n_in(row).wait_recv()
         made = lax.dot_general(
             nb[row], wp[0:256, :], (((1,), (1,)), ((), ())), preferred_element_type=F32
         ).astype(BF)
+        kv[REACH + row, 0:LONGITUDES, :] = made[:, 128:256]
+        kv[REACH + row, LONGITUDES:KEY_COLS, :] = made[0:TILE, 128:256]
+
+        @pl.when(row >= BAND_ROWS - REACH)
+        def _():
+            up_halo(row).start()
+
+        @pl.when(row < REACH)
+        def _():
+            down_halo(row).start()
+
         scaled = made[:, 0:128].astype(F32) * (1.0 / math.sqrt(HEAD_WIDTH))
         q[row, 0:LONGITUDES, :] = scaled
         q[row, LONGITUDES:QUERY_COLS, :] = scaled[0 : TILE // 2]
-        kv[REACH + row, 0:LONGITUDES, :] = made[:, 128:256]
-        kv[REACH + row, LONGITUDES:KEY_COLS, :] = made[0:TILE, 128:256]
-
-    def project_upstream(row):
-        handed_in(ub, suf, ruf, row).wait_recv()
-        made = lax.dot_general(
-            ub[row], wo[0:128, :], (((1,), (1,)), ((), ())), preferred_element_type=F32
-        ).astype(BF)
-        made = made.astype(F32)
-        g[row, 0:LONGITUDES, :] = made
-        g[row, LONGITUDES:QUERY_COLS, :] = made[0 : TILE // 2]
-
-    @pl.loop(1, 8)
-    def _(k):
-        row = chip(k)
-        arrived(nb, sn, rn, row).wait_recv()
-        handed(nb, snf, rnf, row).start()
-        project(chip(k - 1))
-        spread(nb, sn, rn, k).wait_send()
-        spread(ub, su, ru, k).start()
+
+    n_arrived(across).wait_recv()
+    n_out(across).start()
+
+    @pl.loop(1, 4)
+    def _(k):
+        n_passed(k).start()
+
+    w_own(4).start()
+
+    @pl.loop(1, 4)
+    def _(k):
+        w_own(k).start()
+
+    project(me)
+    n_arrived(chip(1)).wait_recv()
+    n_out(chip(1)).start()
+    project(across)
+
+    @pl.loop(3, 8)
+    def _(j):
+        row = chip(j - (1 - j // 5))
+        n_arrived(row).wait_recv()
+        n_out(row).start()
+        project(chip(j - 1 - (1 - (j - 1) // 5)))
+
+        @pl.when(j == 4)
+        def _():
+            w_arrived(across).wait_recv()
+            w_out(across).start()
+
+            @pl.loop(1, 4)
+            def _(k):
+                w_passed(k).start()
 
     project(chip(7))
 
-    up_halo = remote(kv.at[BAND_ROWS : BAND_ROWS + REACH], kv.at[0:REACH], sh.at[0], rh.at[0], along(1))
-    up_halo.start()
-    down_halo = remote(kv.at[REACH : 2 * REACH], kv.at[BAND_ROWS + REACH : KEY_ROWS], sh.at[1], rh.at[1], along(15))
-    down_halo.start()
-
-    @pl.loop(1, 8)
-    def _(k):
-        row = chip(k)
-        arrived(ub, su, ru, row).wait_recv()
-        handed(ub, suf, ruf, row).start()
-        project_upstream(chip(k - 1))
-
-    project_upstream(chip(7))
-    up_halo.wait()
-    down_halo.wait()
+    @pl.loop(1, 4)
+    def _(k):
+        w_arrived(chip(k)).wait_recv()
+        w_out(chip(k)).start()
+        w_arrived(chip(k + 4)).wait_recv()
+        w_out(chip(k + 4)).start()
+
+    @pl.loop(0, 8)
+    def _(k):
+        w_in(k).wait_recv()
+
+    made = lax.dot_general(
+        up_ref[...], wall[...].reshape(WIDTH, WIDTH), (((1,), (1,)), ((), ())), preferred_element_type=F32
+    ).astype(BF)
+    for k in range(8):
+        ds[k] = made[:, k * 128 : (k + 1) * 128]
+
+    def cotangent(k):
+        to = (mp + k) % 16
+        return remote(ds.at[to // 2], gb.at[me, own_half], sd.at[k], rd.at[k], {"mp": to})
+
+    def cotangent_in(k):
+        by = (mp + 16 - k) % 16
+        cut = pl.ds(pl.multiple_of((by % 2) * HALF, HALF), HALF)
+        return remote(gb.at[by // 2, cut], gb.at[by // 2, cut], sd.at[k], rd.at[k], {"mp": by})
+
+    @pl.loop(1, 16)
+    def _(k):
+        cotangent(k).start()
+
+    gb[me, own_half, :] = ds[me]
+    u_own(4).start()
+
+    @pl.loop(1, 4)
+    def _(k):
+        u_own(k).start()
+
+    @pl.loop(1, 16)
+    def _(k):
+        cotangent_in(k).wait_recv()
+
+    lane = lax.broadcasted_iota(jnp.int32, (LONGITUDES, 128), 1)
+
+    @pl.loop(0, BAND_ROWS)
+    def _(row):
+        pair = gb[row].astype(F32)
+        pair = jnp.where(core == 0, pltpu.roll(pair, HEAD_WIDTH, 1), pair)
+        pair = jnp.where(lane < HEAD_WIDTH, 0.0, pair)
+        g[row, 0:LONGITUDES, :] = pair
+        g[row, LONGITUDES:QUERY_COLS, :] = pair[0 : TILE // 2]
+
+    @pl.loop(0, REACH)
+    def _(row):
+        up_halo(row + BAND_ROWS - REACH).wait()
+        down_halo(row).wait()
+
+    def halo_cut(j):
+        return pl.ds(pl.multiple_of(j * 64, 64), 64)
+
+    def down_grad(j):
+        cut = halo_cut(j)
+        return remote(hs.at[0, :, cut], hr.at[0, :, cut], shg.at[j], rhg.at[j], along(15))
+
+    def up_grad(j):
+        cut = halo_cut(j)
+        return remote(hs.at[1, :, cut], hr.at[1, :, cut], shg.at[j + 4], rhg.at[j + 4], along(1))
+
+    def leave(j):
+        cut = pl.ds(pl.multiple_of(j * 64 + TILE, TILE), 64)
+        hs[0, :, halo_cut(j), :] = dkv[0:REACH, cut, :].astype(BF)
+        hs[1, :, halo_cut(j), :] = dkv[BAND_ROWS + REACH : KEY_ROWS, cut, :].astype(BF)
+        down_grad(j).start()
+        up_grad(j).start()
 
     @pl.loop(0, TILES)
     def _(i):
         attention_tile(i, kv, feat_ref, q, g, pick_ref, live_ref, oq, dkv)
 
+        @pl.when((i % 4 == 0) & (i > 0))
+        def _():
+            leave(i // 4 - 1)
+
+        @pl.when(i == 8)
+        def _():
+            u_arrived(across).wait_recv()
+
+            @pl.loop(1, 4)
+            def _(k):
+                u_passed(k).start()
+
+    dkv[:, LONGITUDES:KEY_COLS, :] += dkv[:, :TILE, :]
+    leave(3)
     half = TILE // 2
     oq[:, :half, :] = oq[:, LONGITUDES : LONGITUDES + half, :]
-    dkv[:, :TILE, :] += dkv[:, LONGITUDES : LONGITUDES + TILE, :]
-    hs[0] = dkv[0:REACH, 0:LONGITUDES, :].astype(BF)
-    hs[1] = dkv[BAND_ROWS + REACH : KEY_ROWS, 0:LONGITUDES, :].astype(BF)
-    down_grad = remote(hs.at[0], hr.at[0], shg.at[0], rhg.at[0], along(15))
-    down_grad.start()
-    up_grad = remote(hs.at[1], hr.at[1], shg.at[1], rhg.at[1], along(1))
-    up_grad.start()
     ab[:, :, 0:128] = oq[:, 0:LONGITUDES, :].astype(BF)
-    oq_over = remote(ab.at[:, other_half, 0:128], asib.at[:, :, 0:128], sa.at[0], ra.at[0], sibling)
+    oq_over = remote(ab.at[:, other_half, 0:128], asib.at[:, :, 0:128], sp.at[1], rp.at[1], sibling)
     oq_over.start()
+    weights_over.wait()
+
+    @pl.loop(0, 4)
+    def _(j):
+        down_grad(j).wait()
+        up_grad(j).wait()
+
+    dkv[BAND_ROWS : BAND_ROWS + REACH, TILE:KEY_COLS, :] += hr[0].astype(F32)
+    dkv[REACH : 2 * REACH, TILE:KEY_COLS, :] += hr[1].astype(F32)
+    ab[:, TILE:LONGITUDES, 128:256] = dkv[REACH : REACH + BAND_ROWS, TILE:LONGITUDES, :].astype(BF)
+    ab[:, 0:TILE, 128:256] = dkv[REACH : REACH + BAND_ROWS, LONGITUDES:KEY_COLS, :].astype(BF)
+    kv_over = remote(ab.at[:, other_half, 128:256], asib.at[:, :, 128:256], sp.at[2], rp.at[2], sibling)
+    kv_over.start()
+    oq_over.wait()
+    kv_over.wait()
+
+    def grad_part(row):
+        both = jnp.concatenate([ab[row, own_half, :], asib[row]], axis=1)
+        return jnp.dot(both, wp[...], preferred_element_type=F32)
+
+    def grad_sent(k):
+        row = chip(k)
+        return remote(gs.at[row], gr.at[k // 4 * 4 + x], sgn.at[k], rgn.at[k // 4 * 4 + x], peer(chip(k % 4)))
+
+    def grad_received(k):
+        slot = k // 4 * 4 + chip(k) % 4
+        return remote(gr.at[slot], gr.at[slot], sgn.at[k], rgn.at[slot], peer(chip(k % 4)))
+
+    @pl.loop(1, 8)
+    def _(j):
+        k = (j + 4) % 8
+
+        @pl.when(k % 4 > 0)
+        def _():
+            gs[chip(k)] = grad_part(chip(k)).astype(BF)
+            grad_sent(k).start()
+
+    mine[0] = grad_part(me)
+    mine[1] = grad_part(across)
+
+    low = lax.broadcasted_iota(jnp.int32, (HALF, 128), 1) < HEAD_WIDTH
+
+    @pl.loop(0, BAND_ROWS)
+    def _(row):
+        ours = ab[row, own_half, 0:128].astype(F32)
+        theirs = asib[row, :, 0:128].astype(F32)
+        first = jnp.where(core == 0, ours, theirs)
+        second = jnp.where(core == 0, theirs, ours)
+        os[row] = jnp.where(low, pltpu.roll(first, HEAD_WIDTH, 1), second).astype(BF)
+
+    def heads_sent(k):
+        return remote(os.at[chip(k)], oa.at[me], so.at[k], ro.at[me], peer(chip(k)))
+
+    def heads_received(row):
+        return remote(oa.at[row], oa.at[row], so.at[0], ro.at[row], peer(row))
+
+    @pl.loop(1, 8)
+    def _(k):
+        heads_sent(k).start()
+
+    oa[me] = os[me]
+
+    @pl.loop(1, 4)
+    def _(k):
+        u_arrived(chip(k)).wait_recv()
+        u_arrived(chip(k + 4)).wait_recv()
 
     columns = 512
 
@@ -261,53 +444,15 @@
     def _(n):
         cut = pl.ds(pl.multiple_of(n * columns, columns), columns)
         part = lax.dot_general(
-            ab[:, :, 0:128].reshape(BAND_ROWS * LONGITUDES, 128),
-            ub[:, :, cut].reshape(BAND_ROWS * LONGITUDES, columns),
+            os[...].reshape(BAND_ROWS * HALF, 128),
+            ub[:, :, cut].reshape(BAND_ROWS * HALF, columns),
             (((0,), (0,)), ((), ())),
             preferred_element_type=F32,
         )
-        wg[192:256, cut] = part[64:128]
-
-    out_weights_over.wait()
-    oq_over.wait()
-
-    def sent(buf, into, s, r, k):
-        row = chip(k)
-        return remote(buf.at[row], into.at[me], s.at[k], r.at[me], peer(row))
-
-    def received(into, s, r, row):
-        return remote(into.at[row], into.at[row], s.at[0], r.at[row], peer(row))
-
-    def update_part(row):
-        both = jnp.concatenate([ab[row, own_half, 0:128], asib[row, :, 0:128]], axis=1)
-        return jnp.dot(both, wo[...], preferred_element_type=F32)
-
-    @pl.loop(1, 8)
-    def _(k):
-        us[chip(k)] = update_part(chip(k)).astype(BF)
-        sent(us, ur, sup, rup, k).start()
-
-    mine[0] = update_part(me)
-    down_grad.wait()
-    up_grad.wait()
-    dkv[BAND_ROWS : BAND_ROWS + REACH, 0:LONGITUDES, :] += hr[0].astype(F32)
-    dkv[REACH : 2 * REACH, 0:LONGITUDES, :] += hr[1].astype(F32)
-    ab[:, :, 128:256] = dkv[REACH : REACH + BAND_ROWS, 0:LONGITUDES, :].astype(BF)
-    kv_over = remote(ab.at[:, other_half, 128:256], asib.at[:, :, 128:256], sa.at[1], ra.at[1], sibling)
-    kv_over.start()
-    weights_over.wait()
-    kv_over.wait()
-
-    def grad_part(row):
-        both = jnp.concatenate([ab[row, own_half, :], asib[row]], axis=1)
-        return jnp.dot(both, wp[...], preferred_element_type=F32)
-
-    @pl.loop(1, 8)
-    def _(k):
-        gs[chip(k)] = grad_part(chip(k)).astype(BF)
-        sent(gs, gr, sgn, rgn, k).start()
-
-    mine[1] = grad_part(me)
+        wx[0:2, :, cut] = part.reshape(2, HEAD_WIDTH, columns)
+
+    out_over = remote(wx.at[1 - core], wx.at[2], sp.at[3], rp.at[3], sibling)
+    out_over.start()
 
     @pl.loop(0, WIDTH // columns)
     def _(n):
@@ -321,6 +466,8 @@
         wg[0:64, cut] = part[0:64]
         wg[64:192, cut] = part[128:256]
 
+    out_over.wait()
+    wg[192:256, :] = wx[core] + wx[2]
     wgb[...] = wg[...].astype(BF)
 
     def share(row):
@@ -341,7 +488,23 @@
     def _(k):
         scatter(k).start()
 
-    lr[0] = wgb[share(lat), :]
+    @pl.loop(1, 8)
+    def _(k):
+        heads_received(chip(k)).wait_recv()
+
+    heads = jnp.concatenate([oa[k] for k in range(8)], axis=1)
+    update_ref[...] = jnp.dot(
+        heads, wall[...].reshape(WIDTH, WIDTH), preferred_element_type=F32
+    ).astype(BF)
+
+    total = mine[1]
+    for k in range(5, 8):
+        grad_received(k).wait_recv()
+        total = total + gr[4 + chip(k) % 4].astype(F32)
+    gy[0] = total.astype(BF)
+    over_y = remote(gy.at[0], gy.at[1], sp.at[4], rp.at[4], peer(across))
+    over_y.start()
+
     total = wg[share(lat), :]
     for k in range(1, 16):
         scatter(k).wait()
@@ -353,15 +516,11 @@
         gather(k).start()
 
     total = mine[0]
-    for k in range(1, 8):
-        received(ur, sup, rup, chip(k)).wait_recv()
-        total = total + ur[chip(k)].astype(F32)
-    update_ref[...] = total.astype(BF)
-
-    total = mine[1]
-    for k in range(1, 8):
-        received(gr, sgn, rgn, chip(k)).wait_recv()
-        total = total + gr[chip(k)].astype(F32)
+    for k in range(1, 4):
+        grad_received(k).wait_recv()
+        total = total + gr[chip(k) % 4].astype(F32)
+    over_y.wait()
+    total = total + gy[1].astype(F32)
     features, inverse = normalised()
     centred = features * inverse
     scaled = gain_ref[...] * total
@@ -373,30 +532,44 @@
     def _(k):
         gather(k).wait_send()
         gathered(k).wait_recv()
+        cotangent(k).wait_send()
 
     grad_qkv_ref[...] = lf[0:192, :].astype(F32)
     grad_out_ref[...] = lf[192:256, :].astype(F32)
 
+    @pl.loop(1, 4)
+    def _(k):
+        n_own(k).wait_send()
+        n_passed(k).wait_send()
+        w_own(k).wait_send()
+        w_passed(k).wait_send()
+        u_own(k).wait_send()
+        u_passed(k).wait_send()
+        grad_sent(k).wait_send()
+        grad_sent(k + 4).wait_send()
+
+    n_own(4).wait_send()
+    w_own(4).wait_send()
+    u_own(4).wait_send()
+
     @pl.loop(1, 8)
     def _(k):
-        spread(ub, su, ru, k).wait_send()
-        sent(us, ur, sup, rup, k).wait_send()
-        sent(gs, gr, sgn, rgn, k).wait_send()
+        heads_sent(k).wait_send()
 
     @pl.loop(0, 8)
     def _(k):
-        handed(nb, snf, rnf, k).wait_send()
-        handed(ub, suf, ruf, k).wait_send()
+        n_out(k).wait_send()
+        w_out(k).wait_send()
 
 
 def on_device(tokens, gain, qkv_weight, out_weight, row_cells, upstream):
     band_start = lax.axis_index("lat") * BAND_ROWS
     cells = lax.dynamic_slice_in_dim(jnp.pad(row_cells, (REACH, REACH)), band_start, KEY_ROWS)
-    shape = (BAND_ROWS, LONGITUDES, WIDTH)
     queries = (BAND_ROWS, QUERY_COLS, 128)
     keys = (KEY_ROWS, KEY_COLS, 128)
     halo = (2, REACH, LONGITUDES, 128)
-    blocks = (8, HALF, WIDTH)
+    wide = (8, HALF, WIDTH)
+    pairs = (8, HALF, 128)
     update, grad_input, grad_qkv, grad_out = pl.pallas_call(
         sublayer_kernel,
         out_shape=(
@@ -408,10 +581,10 @@
         in_specs=[pl.BlockSpec(memory_space=VMEM)] * 8,
         out_specs=[pl.BlockSpec(memory_space=VMEM)] * 4,
         scratch_shapes=[
-            VMEM(shape, BF),
-            VMEM(shape, BF),
+            VMEM((BAND_ROWS, LONGITUDES, WIDTH), BF),
+            VMEM(wide, BF),
             VMEM((512, WIDTH), BF),
-            VMEM((256, WIDTH), BF),
+            VMEM((8, 128, WIDTH), BF),
             VMEM(keys, BF),
             VMEM(queries, F32),
             VMEM(queries, F32),
@@ -421,20 +594,23 @@
             VMEM(halo, BF),
             VMEM((BAND_ROWS, LONGITUDES, 256), BF),
             VMEM((BAND_ROWS, HALF, 256), BF),
-            VMEM(blocks, BF),
-            VMEM(blocks, BF),
-            VMEM(blocks, BF),
-            VMEM(blocks, BF),
+            VMEM(pairs, BF),
+            VMEM((BAND_ROWS, LONGITUDES, 128), BF),
+            VMEM(pairs, BF),
+            VMEM(pairs, BF),
+            VMEM(wide, BF),
+            VMEM(wide, BF),
+            VMEM((2, HALF, WIDTH), BF),
             VMEM((2, HALF, WIDTH), F32),
             VMEM((256, WIDTH), F32),
             VMEM((256, WIDTH), BF),
+            VMEM((3, HEAD_WIDTH, WIDTH), F32),
             VMEM((16, 16, WIDTH), BF),
             VMEM((256, WIDTH), BF),
         ]
-        + [DMA((8,))] * 8
-        + [DMA((2,))] * 8
-        + [DMA((8,))] * 4
-        + [DMA((16,))] * 4,
+        + [DMA((8,))] * 20
+        + [DMA((16,))] * 6
+        + [DMA((5,))] * 2,
         compiler_params=pltpu.CompilerParams(
             collective_id=0, has_side_effects=True, vmem_limit_bytes=56 << 20
         ),

time: 194 us -> 145 us (0.75)
  the two profiles are of different devices: /device:TPU:28 before, /device:TPU:2 now
where the time goes in v3:
time: 145 us; the launch traced here: 144 us
  Pallas kernels  133 us (92%)
  local copies, waits for them, and re-layouts  6.21 us (4%)
  other arithmetic  3.64 us (3%)
    pallas_call x1, Pallas kernels, on_device(): pl.pallas_call(sublayer_kernel, out_shape=(jax.ShapeDtypeStruct((HALF, WI...  133 us
    unnamed x8, local copies, waits for them, and re-layouts  5.01 us

profile of v3, /device:TPU:2, one launch (start us, length us, event | category | flops | bytes accessed | tf_op | source)
XLA Modules:
  0.0 144.0 jit_solution(373371442167494917)
XLA Ops:
  0.6 0.7 pad_dynamic-slice_fusion
  1.4 0.1 slice.3
  1.5 0.1 iota.113
  1.6 0.1 iota.114
  1.6 0.1 lt.79
  1.7 0.1 lt.80
  1.8 0.1 iota.120
  1.9 0.7 compare_convert_fusion.live_ref
  2.6 0.8 fusion.16.pick_ref
  3.4 2.1 %select_convert_fusion.feat_ref = bf16[20,272,128]{2,1,0:T(8,128)(2,1)} fusion(s32[128]{0:T(128)S(1)} %get-tuple-element.17, s32[128]{0:T(128)S(1)} %get-tuple-element.16, s32[20]{0:T(128)S(1)} %pad_dynamic-slice_fusion, s32[272]{0:T(512)S(1)} %get-tuple-element.12, s32[272]{0:T(512)S(1)} %get-tuple-element.13, pred[272]{0:T(512)(128)(4,1)S(1)} %fusion.21, ...), kind=kLoop, calls=%fused_computation.6 | loop fusion | flops 20889600 | bytes 1396576 | tf_op jit(solution)/shard_map/convert_element_type | solution.py:44
  5.5 133.5 %sublayer.1 = (bf16[128,1024]{1,0:T(8,128)(2,1)}, bf16[128,1024]{1,0:T(8,128)(2,1)}, f32[192,1024]{1,0:T(8,128)}, f32[64,1024]{1,0:T(8,128)}) custom-call(bf16[128,1024]{1,0:T(8,128)(2,1)} %tok_ref.1, f32[1,1024]{1,0:T(1,128)} %bitcast.9, bf16[192,1024]{1,0:T(8,128)(2,1)} %bitcast.6, bf16[64,1024]{1,0:T(8,128)(2,1)} %bitcast.8, bf16[128,1024]{1,0:T(8,128)(2,1)} %up_ref.1, ...), custom_call_target="tpu_custom_call" | custom-call | tf_op jit(solution)/shard_map/sublayer/pallas_call | solution.py:573
  139.0 0.0 copy-start
  139.0 0.0 copy-start.1
  139.0 1.8 %copy.14 = bf16[128,1024]{1,0:T(8,128)(2,1)} copy(bf16[128,1024]{1,0:T(8,128)(2,1)} %get-tuple-element.22) | data formatting | bytes 524288
  140.8 1.7 %copy.15 = bf16[128,1024]{1,0:T(8,128)(2,1)} copy(bf16[128,1024]{1,0:T(8,128)(2,1)} %get-tuple-element.23) | data formatting | bytes 524288
  142.5 0.0 copy-done
  142.5 0.9 copy.16
  143.3 0.0 copy-done.1
  143.3 0.7 copy.17
  (9 shorter events, 0.0 us)
Async XLA Ops:
  139.0 3.4 %copy-start = (f32[192,1024]{1,0:T(8,128)S(1)}, f32[192,1024]{1,0:T(8,128)}, u32[]{:S(2)}) copy-start(f32[192,1024]{1,0:T(8,128)} %get-tuple-element.10) | copy-start | bytes 2359300
  139.0 4.3 %copy-start.1 = (f32[64,1024]{1,0:T(8,128)S(1)}, f32[64,1024]{1,0:T(8,128)}, u32[]{:S(2)}) copy-start(f32[64,1024]{1,0:T(8,128)} %get-tuple-element.11) | copy-start | bytes 786436

commit v4 on v3

--- a/solution.py
+++ b/solution.py
@@ -27,43 +27,34 @@
 DMA = pltpu.SemaphoreType.DMA
 
 
-def key_features(cells):
-    shape = (KEY_ROWS, KEY_COLS, 128)
-    row = lax.broadcasted_iota(jnp.int32, shape, 0)
-    col = lax.broadcasted_iota(jnp.int32, shape, 1)
-    lane = lax.broadcasted_iota(jnp.int32, shape, 2)
-    live = col % LONGITUDES < cells[:, None, None]
+def row_features(row, cells):
+    shape = (KEY_COLS, 128)
+    col = lax.broadcasted_iota(jnp.int32, shape, 0)
+    lane = lax.broadcasted_iota(jnp.int32, shape, 1)
+    live = (col & (LONGITUDES - 1)) < cells
     near_row = (row >= lane - 8) & (row <= lane - 8 + 2 * REACH)
-    apart = (col - lane) % 32
+    apart = (col - lane) & 31
     near_col = (apart <= REACH) | (apart >= 32 - REACH)
     barred = (
         ((lane == 0) & ~live)
         | ((lane >= 8) & (lane < 16) & ~near_row)
         | ((lane >= 32) & (lane < 64) & ~near_col)
     )
-    return jnp.where(barred, NEVER, 0.0).astype(jnp.bfloat16)
-
-
-def query_features():
-    shape = (2, BAND_ROWS, TILE, 128)
-    tile, row, col, lane = (lax.broadcasted_iota(jnp.int32, shape, d) for d in range(4))
+    return jnp.where(barred, NEVER, 0.0).astype(BF)
+
+
+def query_features(parity):
+    shape = (BAND_ROWS, TILE, 128)
+    row, col, lane = (lax.broadcasted_iota(jnp.int32, shape, d) for d in range(3))
     picked = (
         (lane == 0)
         | (lane == 8 + row)
-        | (lane == 32 + (TILE * tile + TILE // 2 + col) % 32)
-    )
-    return picked.astype(jnp.bfloat16).reshape(2, BAND_ROWS * TILE, 128)
-
-
-def live_queries(cells):
-    shape = (TILES, 1, BAND_ROWS, TILE)
-    tile, _, _, col = (lax.broadcasted_iota(jnp.int32, shape, d) for d in range(4))
-    at = (TILE * tile + TILE // 2 + col) % LONGITUDES
-    live = at < cells[REACH : REACH + BAND_ROWS][None, None, :, None]
-    return live.astype(jnp.float32).reshape(TILES, 1, BAND_ROWS * TILE)
-
-
-def attention_tile(i, kv_ref, feat_ref, q_ref, g_ref, pick_ref, live_ref, oq_ref, dkv_ref):
+        | (lane == 32 + ((TILE * parity + TILE // 2 + col) & 31))
+    )
+    return jnp.where(picked, 1.0, 0.0).reshape(BAND_ROWS * TILE, 128).astype(BF)
+
+
+def attention_tile(i, kv_ref, feat_ref, q_ref, g_ref, pick_ref, cells, oq_ref, dkv_ref):
     queries = BAND_ROWS * TILE
     keys = KEY_ROWS * WINDOW
     c0 = pl.multiple_of(i * TILE, TILE)
@@ -90,7 +81,10 @@
     grad_probs = products[:, queries:]
     highest = jnp.max(scores, axis=0, keepdims=True)
     terms = jnp.exp(scores - highest)
-    probs = terms * (live_ref[i] / jnp.sum(terms, axis=0, keepdims=True))
+    query = lax.broadcasted_iota(jnp.int32, (1, queries), 1)
+    col = (i * TILE + TILE // 2 + (query & (TILE - 1))) & (LONGITUDES - 1)
+    live = jnp.where(col < cells, 1.0, 0.0)
+    probs = terms * (live / jnp.sum(terms, axis=0, keepdims=True))
     weights = probs.astype(jnp.bfloat16)
     row_delta = jnp.sum(probs * grad_probs, axis=0, keepdims=True)
     grad_scores = (probs * (grad_probs - row_delta)).astype(jnp.bfloat16)
@@ -117,9 +111,9 @@
 
 
 def sublayer_kernel(
-    tok_ref, gain_ref, w_ref, wo_ref, up_ref, feat_ref, pick_ref, live_ref,
-    update_ref, grad_in_ref, grad_qkv_ref, grad_out_ref,
-    nb, ub, wp, wall, kv, q, g, oq, dkv, hs, hr, ab, asib, ds, gb, os, oa, gs, gr, gy, mine, wg, wgb, wx, lr, lf,
+    tok_ref, gain_ref, w_ref, wo_ref, up_ref, cells_ref,
+    update_ref, grad_in_ref, grads_ref,
+    feat, pick, nb, ub, wp, wall, kv, q, g, oq, dkv, hs, hr, ab, asib, ds, gb, os, oa, gs, gr, gy, mine, wg, wgb, wx, lr, lf,
     sn, rn, snf, rnf, su, ru, sw, rw, swf, rwf, sku, rku, skd, rkd, shg, rhg, so, ro, sgn, rgn,
     sd, rd, sl, rl, sf, rf, sp, rp,
 ):
@@ -170,20 +164,21 @@
     wp[128:256, :] = w_ref[64:192, :]
     pl.semaphore_wait(barrier, 30)
 
-    def blocks(buf, cut, s, r):
-        def at(row):
-            return buf.at[row] if cut is None else buf.at[row, cut]
-
-        def own(k):
-            return remote(at(me), at(me), s.at[k], r.at[me], peer(chip(k)))
-
-        def passed(k):
-            return remote(at(across), at(across), s.at[k + 4], r.at[across], peer(chip(k)))
-
-        def arrived(row):
-            return remote(at(row), at(row), s.at[0], r.at[row], peer(row))
-
-        return own, passed, arrived
+    east, west, opposite = chip(1), chip(2), chip(3)
+    across_east, across_west, across_opposite = chip(5), chip(6), chip(7)
+
+    class Gather:
+        def __init__(self, buf, cut, s, r):
+            self.at = lambda row: buf.at[row] if cut is None else buf.at[row, cut]
+            self.s, self.r = s, r
+
+        def move(self, i):
+            block = (me, me, me, across, across, west, across_east)[i]
+            to = (across, east, west, east, west, east, west)[i]
+            return remote(self.at(block), self.at(block), self.s.at[i], self.r.at[block], peer(to))
+
+        def arrive(self, row):
+            remote(self.at(row), self.at(row), self.s.at[0], self.r.at[row], peer(row)).wait_recv()
 
     def handing(buf, cut, cut_in, s, r):
         def out(row):
@@ -194,23 +189,38 @@
 
         return out, into
 
-    n_own, n_passed, n_arrived = blocks(nb, own_half, sn, rn)
+    n_gather = Gather(nb, own_half, sn, rn)
     n_out, n_in = handing(nb, own_half, other_half, snf, rnf)
-    w_own, w_passed, w_arrived = blocks(wall, own_head, sw, rw)
+    w_gather = Gather(wall, own_head, sw, rw)
     w_out, w_in = handing(wall, own_head, other_head, swf, rwf)
-    u_own, u_passed, u_arrived = blocks(ub, None, su, ru)
-
-    n_own(4).start()
-
-    @pl.loop(1, 4)
-    def _(k):
-        n_own(k).start()
-
+    u_gather = Gather(ub, None, su, ru)
+
+    for i in range(3):
+        w_gather.move(i).start()
+    for i in range(3):
+        n_gather.move(i).start()
+    u_gather.move(0).start()
+    w_out(me).start()
     n_out(me).start()
-    w_out(me).start()
     weights_over = remote(wp.at[0:256], wp.at[256:512], sp.at[0], rp.at[0], sibling)
     weights_over.start()
+
+    def cells_of(row):
+        inside = (row >= 0) & (row < 128)
+        return jnp.where(inside, cells_ref[jnp.clip(row, 0, 127)], 0)
+
     dkv[...] = jnp.zeros_like(dkv)
+
+    @pl.loop(0, KEY_ROWS)
+    def _(row):
+        feat[row] = row_features(row, cells_of(lat * BAND_ROWS + row - REACH))
+
+    pick[0] = query_features(0)
+    pick[1] = query_features(1)
+    query_row = lax.broadcasted_iota(jnp.int32, (1, BAND_ROWS * TILE), 1) // TILE
+    query_cells = jnp.zeros((1, BAND_ROWS * TILE), jnp.int32)
+    for r in range(BAND_ROWS):
+        query_cells = jnp.where(query_row == r, cells_of(lat * BAND_ROWS + r), query_cells)
 
     def up_halo(row):
         return remote(kv.at[REACH + row], kv.at[row + REACH - BAND_ROWS], sku.at[row], rku.at[row], along(1))
@@ -238,48 +248,22 @@
         q[row, 0:LONGITUDES, :] = scaled
         q[row, LONGITUDES:QUERY_COLS, :] = scaled[0 : TILE // 2]
 
-    n_arrived(across).wait_recv()
-    n_out(across).start()
-
-    @pl.loop(1, 4)
-    def _(k):
-        n_passed(k).start()
-
-    w_own(4).start()
-
-    @pl.loop(1, 4)
-    def _(k):
-        w_own(k).start()
-
+    def passed_on(gather, out, row, moves):
+        gather.arrive(row)
+        for i in moves:
+            gather.move(i).start()
+        out(row).start()
+
+    passed_on(w_gather, w_out, west, (5,))
+    passed_on(w_gather, w_out, across, (3, 4))
+    passed_on(n_gather, n_out, west, (5,))
+    passed_on(n_gather, n_out, across, (3, 4))
+    passed_on(w_gather, w_out, across_east, (6,))
     project(me)
-    n_arrived(chip(1)).wait_recv()
-    n_out(chip(1)).start()
-    project(across)
-
-    @pl.loop(3, 8)
-    def _(j):
-        row = chip(j - (1 - j // 5))
-        n_arrived(row).wait_recv()
-        n_out(row).start()
-        project(chip(j - 1 - (1 - (j - 1) // 5)))
-
-        @pl.when(j == 4)
-        def _():
-            w_arrived(across).wait_recv()
-            w_out(across).start()
-
-            @pl.loop(1, 4)
-            def _(k):
-                w_passed(k).start()
-
-    project(chip(7))
-
-    @pl.loop(1, 4)
-    def _(k):
-        w_arrived(chip(k)).wait_recv()
-        w_out(chip(k)).start()
-        w_arrived(chip(k + 4)).wait_recv()
-        w_out(chip(k + 4)).start()
+    for row in (east, across_west, opposite, across_opposite):
+        passed_on(w_gather, w_out, row, ())
+    passed_on(n_gather, n_out, across_east, (6,))
+    passed_on(n_gather, n_out, east, ())
 
     @pl.loop(0, 8)
     def _(k):
@@ -305,11 +289,23 @@
         cotangent(k).start()
 
     gb[me, own_half, :] = ds[me]
-    u_own(4).start()
-
-    @pl.loop(1, 4)
-    def _(k):
-        u_own(k).start()
+
+    @pl.loop(0, 7)
+    def _(j):
+        k = jnp.where(j == 0, 2, jnp.where(j == 1, 4, jnp.where(j == 2, 1, jnp.where(j == 3, 5, 0))))
+        k = jnp.where(j == 4, 3, jnp.where(j == 5, 6, jnp.where(j == 6, 7, k)))
+
+        @pl.when(j < 3)
+        def _():
+            later = jnp.where(j == 0, 3, jnp.where(j == 1, 6, 7))
+            n_gather.arrive(chip(later))
+            n_out(chip(later)).start()
+
+        project(chip(k))
+
+    u_gather.arrive(across)
+    for i in (1, 2, 3, 4):
+        u_gather.move(i).start()
 
     @pl.loop(1, 16)
     def _(k):
@@ -350,19 +346,18 @@
 
     @pl.loop(0, TILES)
     def _(i):
-        attention_tile(i, kv, feat_ref, q, g, pick_ref, live_ref, oq, dkv)
+        attention_tile(i, kv, feat, q, g, pick, query_cells, oq, dkv)
 
         @pl.when((i % 4 == 0) & (i > 0))
         def _():
             leave(i // 4 - 1)
 
-        @pl.when(i == 8)
+        @pl.when(i == 10)
         def _():
-            u_arrived(across).wait_recv()
-
-            @pl.loop(1, 4)
-            def _(k):
-                u_passed(k).start()
+            u_gather.arrive(west)
+            u_gather.move(5).start()
+            u_gather.arrive(across_east)
+            u_gather.move(6).start()
 
     dkv[:, LONGITUDES:KEY_COLS, :] += dkv[:, :TILE, :]
     leave(3)
@@ -391,25 +386,14 @@
         both = jnp.concatenate([ab[row, own_half, :], asib[row]], axis=1)
         return jnp.dot(both, wp[...], preferred_element_type=F32)
 
-    def grad_sent(k):
-        row = chip(k)
-        return remote(gs.at[row], gr.at[k // 4 * 4 + x], sgn.at[k], rgn.at[k // 4 * 4 + x], peer(chip(k % 4)))
-
-    def grad_received(k):
-        slot = k // 4 * 4 + chip(k) % 4
-        return remote(gr.at[slot], gr.at[slot], sgn.at[k], rgn.at[slot], peer(chip(k % 4)))
-
-    @pl.loop(1, 8)
-    def _(j):
-        k = (j + 4) % 8
-
-        @pl.when(k % 4 > 0)
-        def _():
-            gs[chip(k)] = grad_part(chip(k)).astype(BF)
-            grad_sent(k).start()
-
-    mine[0] = grad_part(me)
-    mine[1] = grad_part(across)
+    def grad_sent(i):
+        to = (east, west, west, east, east, west)[i]
+        return remote(gs.at[i], gr.at[i], sgn.at[i], rgn.at[i], peer(to))
+
+    gs[1] = grad_part(across_opposite).astype(BF)
+    grad_sent(1).start()
+    gs[0] = grad_part(opposite).astype(BF)
+    grad_sent(0).start()
 
     low = lax.broadcasted_iota(jnp.int32, (HALF, 128), 1) < HEAD_WIDTH
 
@@ -433,10 +417,8 @@
 
     oa[me] = os[me]
 
-    @pl.loop(1, 4)
-    def _(k):
-        u_arrived(chip(k)).wait_recv()
-        u_arrived(chip(k + 4)).wait_recv()
+    for row in (east, across_west, opposite, across_opposite):
+        u_gather.arrive(row)
 
     columns = 512
 
@@ -488,22 +470,30 @@
     def _(k):
         scatter(k).start()
 
-    @pl.loop(1, 8)
-    def _(k):
-        heads_received(chip(k)).wait_recv()
-
-    heads = jnp.concatenate([oa[k] for k in range(8)], axis=1)
-    update_ref[...] = jnp.dot(
-        heads, wall[...].reshape(WIDTH, WIDTH), preferred_element_type=F32
-    ).astype(BF)
-
-    total = mine[1]
-    for k in range(5, 8):
-        grad_received(k).wait_recv()
-        total = total + gr[4 + chip(k) % 4].astype(F32)
-    gy[0] = total.astype(BF)
+    grad_sent(1).wait_recv()
+    gs[2] = (grad_part(across_west) + gr[1].astype(F32)).astype(BF)
+    grad_sent(2).start()
+    gs[3] = grad_part(across_east).astype(BF)
+    grad_sent(3).start()
+    grad_sent(0).wait_recv()
+    gs[4] = (grad_part(east) + gr[0].astype(F32)).astype(BF)
+    grad_sent(4).start()
+    gs[5] = grad_part(west).astype(BF)
+    grad_sent(5).start()
+    mine[0] = grad_part(me)
+    mine[1] = grad_part(across)
+    grad_sent(2).wait_recv()
+    grad_sent(3).wait_recv()
+    gy[0] = (mine[1] + gr[2].astype(F32) + gr[3].astype(F32)).astype(BF)
     over_y = remote(gy.at[0], gy.at[1], sp.at[4], rp.at[4], peer(across))
     over_y.start()
+
+    @pl.loop(1, 8)
+    def _(k):
+        heads_received(chip(k)).wait_recv()
+
+    heads = jnp.concatenate([oa[k] for k in range(8)], axis=1)
+    update_ref[...] = jnp.dot(heads, wall[...].reshape(WIDTH, WIDTH), preferred_element_type=F32)
 
     total = wg[share(lat), :]
     for k in range(1, 16):
@@ -515,18 +505,17 @@
     def _(k):
         gather(k).start()
 
-    total = mine[0]
-    for k in range(1, 4):
-        grad_received(k).wait_recv()
-        total = total + gr[chip(k) % 4].astype(F32)
+    grad_sent(4).wait_recv()
+    grad_sent(5).wait_recv()
+    total = mine[0] + gr[4].astype(F32) + gr[5].astype(F32)
     over_y.wait()
     total = total + gy[1].astype(F32)
     features, inverse = normalised()
     centred = features * inverse
     scaled = gain_ref[...] * total
-    grad_in_ref[...] = (
-        inverse * (scaled - centred * jnp.mean(scaled * centred, axis=1, keepdims=True))
-    ).astype(BF)
+    grad_in_ref[...] = inverse * (
+        scaled - centred * jnp.mean(scaled * centred, axis=1, keepdims=True)
+    )
 
     @pl.loop(1, 16)
     def _(k):
@@ -534,23 +523,14 @@
         gathered(k).wait_recv()
         cotangent(k).wait_send()
 
-    grad_qkv_ref[...] = lf[0:192, :].astype(F32)
-    grad_out_ref[...] = lf[192:256, :].astype(F32)
-
-    @pl.loop(1, 4)
-    def _(k):
-        n_own(k).wait_send()
-        n_passed(k).wait_send()
-        w_own(k).wait_send()
-        w_passed(k).wait_send()
-        u_own(k).wait_send()
-        u_passed(k).wait_send()
-        grad_sent(k).wait_send()
-        grad_sent(k + 4).wait_send()
-
-    n_own(4).wait_send()
-    w_own(4).wait_send()
-    u_own(4).wait_send()
+    grads_ref[...] = lf[...]
+
+    for i in range(7):
+        n_gather.move(i).wait_send()
+        w_gather.move(i).wait_send()
+        u_gather.move(i).wait_send()
+    for i in range(6):
+        grad_sent(i).wait_send()
 
     @pl.loop(1, 8)
     def _(k):
@@ -563,24 +543,23 @@
 
 
 def on_device(tokens, gain, qkv_weight, out_weight, row_cells, upstream):
-    band_start = lax.axis_index("lat") * BAND_ROWS
-    cells = lax.dynamic_slice_in_dim(jnp.pad(row_cells, (REACH, REACH)), band_start, KEY_ROWS)
     queries = (BAND_ROWS, QUERY_COLS, 128)
     keys = (KEY_ROWS, KEY_COLS, 128)
     halo = (2, REACH, LONGITUDES, 128)
     wide = (8, HALF, WIDTH)
     pairs = (8, HALF, 128)
-    update, grad_input, grad_qkv, grad_out = pl.pallas_call(
+    update, grad_input, grads = pl.pallas_call(
         sublayer_kernel,
         out_shape=(
-            jax.ShapeDtypeStruct((HALF, WIDTH), BF),
-            jax.ShapeDtypeStruct((HALF, WIDTH), BF),
-            jax.ShapeDtypeStruct((3 * HEAD_WIDTH, WIDTH), F32),
-            jax.ShapeDtypeStruct((HEAD_WIDTH, WIDTH), F32),
+            jax.ShapeDtypeStruct((HALF, WIDTH), F32),
+            jax.ShapeDtypeStruct((HALF, WIDTH), F32),
+            jax.ShapeDtypeStruct((256, WIDTH), BF),
         ),
-        in_specs=[pl.BlockSpec(memory_space=VMEM)] * 8,
-        out_specs=[pl.BlockSpec(memory_space=VMEM)] * 4,
+        in_specs=[pl.BlockSpec(memory_space=VMEM)] * 5 + [pl.BlockSpec(memory_space=pltpu.SMEM)],
+        out_specs=[pl.BlockSpec(memory_space=VMEM)] * 3,
         scratch_shapes=[
+            VMEM(keys, BF),
+            VMEM((2, BAND_ROWS * TILE, 128), BF),
             VMEM((BAND_ROWS, LONGITUDES, WIDTH), BF),
             VMEM(wide, BF),
             VMEM((512, WIDTH), BF),
@@ -621,15 +600,14 @@
         qkv_weight.reshape(3 * HEAD_WIDTH, WIDTH),
         out_weight.reshape(HEAD_WIDTH, WIDTH),
         upstream,
-        key_features(cells),
-        query_features(),
-        live_queries(cells),
-    )
+        row_cells,
+    )
+    grads = grads.astype(F32)
     return (
-        update,
-        grad_input,
-        grad_qkv.reshape(1, 3 * HEAD_WIDTH, WIDTH),
-        grad_out.reshape(1, HEAD_WIDTH, WIDTH),
+        update.astype(BF),
+        grad_input.astype(BF),
+        grads[0 : 3 * HEAD_WIDTH].reshape(1, 3 * HEAD_WIDTH, WIDTH),
+        grads[3 * HEAD_WIDTH :].reshape(1, HEAD_WIDTH, WIDTH),
     )
 
 

time: 145 us -> 125 us (0.86)
  Pallas kernels: 133 us -> 118 us
  local copies, waits for them, and re-layouts: 6.21 us -> 2.06 us
    pallas_call x1, Pallas kernels: 133 us -> 118 us  [on_device(): pl.pallas_call(sublayer_kernel, out_shape=(jax.ShapeDtypeStruct((HALF, WI...]
    unnamed x8 -> x4, local copies, waits for them, and re-layouts: 5.01 us -> 0.4 us
    reshape x0 -> x2, local copies, waits for them, and re-layouts: none -> 1.66 us  [the longest x1 0.93 us: on_device(): grads[0:3 * HEAD_WIDTH].reshape(1, 3 * HEAD_WIDTH, WIDTH)]
where the time goes in v4:
time: 125 us; the launch traced here: 124 us
  Pallas kernels  118 us (94%)
  other arithmetic  2.68 us (2%)
  local copies, waits for them, and re-layouts  2.06 us (2%)
    pallas_call x1, Pallas kernels, on_device(): pl.pallas_call(sublayer_kernel, out_shape=(jax.ShapeDtypeStruct((HALF, WI...  118 us

profile of v4, /device:TPU:2, one launch (start us, length us, event | category | flops | bytes accessed | tf_op | source)
XLA Modules:
  0.0 123.8 jit_solution(3058296838646362552)
XLA Ops:
  0.6 118.4 %sublayer.1 = (f32[128,1024]{1,0:T(8,128)}, f32[128,1024]{1,0:T(8,128)}, bf16[256,1024]{1,0:T(8,128)(2,1)}) custom-call(bf16[128,1024]{1,0:T(8,128)(2,1)} %tok_ref.1, f32[1,1024]{1,0:T(1,128)} %bitcast.9, bf16[192,1024]{1,0:T(8,128)(2,1)} %bitcast.7, bf16[64,1024]{1,0:T(8,128)(2,1)} %bitcast.8, bf16[128,1024]{1,0:T(8,128)(2,1)} %up_ref.1, s32[128]{0:T(128)} %cells_ref.1), custom_call_target="tpu_custom_call" | custom-call | tf_op jit(solution)/shard_map/sublayer/pallas_call | solution.py:551
  119.1 0.0 copy-start.1
  119.1 1.8 %convert_element_type.9 = bf16[128,1024]{1,0:T(8,128)(2,1)} convert(f32[128,1024]{1,0:T(8,128)} %get-tuple-element.7) | non-fusion elementwise | flops 131072 | bytes 786432 | tf_op jit(solution)/shard_map/convert_element_type | solution.py:607
  120.9 0.0 copy-done.1
  120.9 0.0 copy-start
  120.9 0.7 convert_element_type.10
  121.7 0.4 copy-done
  122.1 0.1 convert_element_type.11
  122.2 0.7 slice_bitcast_fusion.1
  122.9 0.9 slice_bitcast_fusion
Async XLA Ops:
  119.1 1.8 %copy-start.1 = (f32[128,1024]{1,0:T(8,128)S(1)}, f32[128,1024]{1,0:T(8,128)}, u32[]{:S(2)}) copy-start(f32[128,1024]{1,0:T(8,128)} %get-tuple-element.8) | copy-start | bytes 1572868
  120.9 1.1 copy-start

commit v5 on v4

--- a/solution.py
+++ b/solution.py
@@ -196,12 +196,11 @@
     u_gather = Gather(ub, None, su, ru)
 
     for i in range(3):
+        n_gather.move(i).start()
+    n_out(me).start()
+    for i in range(3):
         w_gather.move(i).start()
-    for i in range(3):
-        n_gather.move(i).start()
-    u_gather.move(0).start()
     w_out(me).start()
-    n_out(me).start()
     weights_over = remote(wp.at[0:256], wp.at[256:512], sp.at[0], rp.at[0], sibling)
     weights_over.start()
 
@@ -222,11 +221,14 @@
     for r in range(BAND_ROWS):
         query_cells = jnp.where(query_row == r, cells_of(lat * BAND_ROWS + r), query_cells)
 
+    def whole(row):
+        return kv.at[row, 0:LONGITUDES]
+
     def up_halo(row):
-        return remote(kv.at[REACH + row], kv.at[row + REACH - BAND_ROWS], sku.at[row], rku.at[row], along(1))
+        return remote(whole(REACH + row), whole(row + REACH - BAND_ROWS), sku.at[row], rku.at[row], along(1))
 
     def down_halo(row):
-        return remote(kv.at[REACH + row], kv.at[row + REACH + BAND_ROWS], skd.at[row], rkd.at[row], along(15))
+        return remote(whole(REACH + row), whole(row + REACH + BAND_ROWS), skd.at[row], rkd.at[row], along(15))
 
     def project(row):
         n_in(row).wait_recv()
@@ -254,80 +256,90 @@
             gather.move(i).start()
         out(row).start()
 
+    def cotangent(row, c):
+        k = row * 2 + c
+        return remote(ds.at[row], gb.at[me, own_half], sd.at[k], rd.at[mp], {"mp": k})
+
+    def cotangent_in(row, c):
+        cut = pl.ds(c * HALF, HALF)
+        k = row * 2 + c
+        return remote(gb.at[row, cut], gb.at[row, cut], sd.at[k], rd.at[k], {"mp": k})
+
+    def cotangents(row):
+        w_in(row).wait_recv()
+        ds[row] = lax.dot_general(
+            up_ref[...], wall[row], (((1,), (1,)), ((), ())), preferred_element_type=F32
+        ).astype(BF)
+        cotangent(row, 0).start()
+        cotangent(row, 1).start()
+
+    project(me)
+    passed_on(n_gather, n_out, west, (5,))
+    passed_on(n_gather, n_out, across, (3, 4))
     passed_on(w_gather, w_out, west, (5,))
     passed_on(w_gather, w_out, across, (3, 4))
-    passed_on(n_gather, n_out, west, (5,))
-    passed_on(n_gather, n_out, across, (3, 4))
+    passed_on(n_gather, n_out, east, ())
+    project(west)
+    project(across)
+    passed_on(n_gather, n_out, across_east, (6,))
     passed_on(w_gather, w_out, across_east, (6,))
-    project(me)
-    for row in (east, across_west, opposite, across_opposite):
-        passed_on(w_gather, w_out, row, ())
-    passed_on(n_gather, n_out, across_east, (6,))
-    passed_on(n_gather, n_out, east, ())
-
-    @pl.loop(0, 8)
-    def _(k):
-        w_in(k).wait_recv()
-
-    made = lax.dot_general(
-        up_ref[...], wall[...].reshape(WIDTH, WIDTH), (((1,), (1,)), ((), ())), preferred_element_type=F32
+    project(east)
+    passed_on(n_gather, n_out, opposite, ())
+    project(across_east)
+    passed_on(n_gather, n_out, across_west, ())
+    project(opposite)
+    passed_on(w_gather, w_out, east, ())
+    passed_on(w_gather, w_out, across_west, ())
+    cotangents(west)
+    cotangents(across)
+    cotangents(across_east)
+    passed_on(n_gather, n_out, across_opposite, ())
+    project(across_west)
+    passed_on(w_gather, w_out, opposite, ())
+    passed_on(w_gather, w_out, across_opposite, ())
+    cotangents(east)
+    cotangents(across_west)
+    cotangents(opposite)
+    project(across_opposite)
+    cotangents(across_opposite)
+    w_in(me).wait_recv()
+    ds[me] = lax.dot_general(
+        up_ref[...], wall[me], (((1,), (1,)), ((), ())), preferred_element_type=F32
     ).astype(BF)
-    for k in range(8):
-        ds[k] = made[:, k * 128 : (k + 1) * 128]
-
-    def cotangent(k):
-        to = (mp + k) % 16
-        return remote(ds.at[to // 2], gb.at[me, own_half], sd.at[k], rd.at[k], {"mp": to})
-
-    def cotangent_in(k):
-        by = (mp + 16 - k) % 16
-        cut = pl.ds(pl.multiple_of((by % 2) * HALF, HALF), HALF)
-        return remote(gb.at[by // 2, cut], gb.at[by // 2, cut], sd.at[k], rd.at[k], {"mp": by})
-
-    @pl.loop(1, 16)
-    def _(k):
-        cotangent(k).start()
-
+    home = remote(ds.at[me], gb.at[me, own_half], sp.at[5], rp.at[5], sibling)
+    home.start()
     gb[me, own_half, :] = ds[me]
-
-    @pl.loop(0, 7)
-    def _(j):
-        k = jnp.where(j == 0, 2, jnp.where(j == 1, 4, jnp.where(j == 2, 1, jnp.where(j == 3, 5, 0))))
-        k = jnp.where(j == 4, 3, jnp.where(j == 5, 6, jnp.where(j == 6, 7, k)))
-
-        @pl.when(j < 3)
-        def _():
-            later = jnp.where(j == 0, 3, jnp.where(j == 1, 6, 7))
-            n_gather.arrive(chip(later))
-            n_out(chip(later)).start()
-
-        project(chip(k))
-
-    u_gather.arrive(across)
-    for i in (1, 2, 3, 4):
+    for i in range(3):
         u_gather.move(i).start()
 
-    @pl.loop(1, 16)
-    def _(k):
-        cotangent_in(k).wait_recv()
-
     lane = lax.broadcasted_iota(jnp.int32, (LONGITUDES, 128), 1)
 
-    @pl.loop(0, BAND_ROWS)
-    def _(row):
+    def cotangent_rows(row):
         pair = gb[row].astype(F32)
         pair = jnp.where(core == 0, pltpu.roll(pair, HEAD_WIDTH, 1), pair)
         pair = jnp.where(lane < HEAD_WIDTH, 0.0, pair)
         g[row, 0:LONGITUDES, :] = pair
         g[row, LONGITUDES:QUERY_COLS, :] = pair[0 : TILE // 2]
 
+    @pl.loop(1, 8)
+    def _(k):
+        cotangent_in(chip(k), 0).wait_recv()
+        cotangent_in(chip(k), 1).wait_recv()
+        cotangent_rows(chip(k))
+
+    home.wait()
+    cotangent_rows(me)
+
     @pl.loop(0, REACH)
     def _(row):
         up_halo(row + BAND_ROWS - REACH).wait()
         down_halo(row).wait()
 
+    kv[0:REACH, LONGITUDES:KEY_COLS, :] = kv[0:REACH, 0:TILE, :]
+    kv[BAND_ROWS + REACH : KEY_ROWS, LONGITUDES:KEY_COLS, :] = kv[BAND_ROWS + REACH : KEY_ROWS, 0:TILE, :]
+
     def halo_cut(j):
-        return pl.ds(pl.multiple_of(j * 64, 64), 64)
+        return pl.ds(pl.multiple_of(j * WINDOW, WINDOW), WINDOW)
 
     def down_grad(j):
         cut = halo_cut(j)
@@ -335,10 +347,10 @@
 
     def up_grad(j):
         cut = halo_cut(j)
-        return remote(hs.at[1, :, cut], hr.at[1, :, cut], shg.at[j + 4], rhg.at[j + 4], along(1))
+        return remote(hs.at[1, :, cut], hr.at[1, :, cut], shg.at[j + 8], rhg.at[j + 8], along(1))
 
     def leave(j):
-        cut = pl.ds(pl.multiple_of(j * 64 + TILE, TILE), 64)
+        cut = pl.ds(pl.multiple_of(j * WINDOW + TILE, TILE), WINDOW)
         hs[0, :, halo_cut(j), :] = dkv[0:REACH, cut, :].astype(BF)
         hs[1, :, halo_cut(j), :] = dkv[BAND_ROWS + REACH : KEY_ROWS, cut, :].astype(BF)
         down_grad(j).start()
@@ -348,52 +360,49 @@
     def _(i):
         attention_tile(i, kv, feat, q, g, pick, query_cells, oq, dkv)
 
-        @pl.when((i % 4 == 0) & (i > 0))
+        @pl.when((i % 2 == 0) & (i > 0))
         def _():
-            leave(i // 4 - 1)
-
-        @pl.when(i == 10)
+            leave(i // 2 - 1)
+
+        @pl.when(i == 6)
+        def _():
+            u_gather.arrive(across)
+            u_gather.move(3).start()
+            u_gather.move(4).start()
+
+        @pl.when(i == 8)
         def _():
             u_gather.arrive(west)
             u_gather.move(5).start()
+
+        @pl.when(i == 13)
+        def _():
             u_gather.arrive(across_east)
             u_gather.move(6).start()
 
     dkv[:, LONGITUDES:KEY_COLS, :] += dkv[:, :TILE, :]
-    leave(3)
+    leave(7)
     half = TILE // 2
     oq[:, :half, :] = oq[:, LONGITUDES : LONGITUDES + half, :]
     ab[:, :, 0:128] = oq[:, 0:LONGITUDES, :].astype(BF)
     oq_over = remote(ab.at[:, other_half, 0:128], asib.at[:, :, 0:128], sp.at[1], rp.at[1], sibling)
     oq_over.start()
+
+    columns = 512
+
+    @pl.loop(0, WIDTH // columns)
+    def _(n):
+        cut = pl.ds(pl.multiple_of(n * columns, columns), columns)
+        part = lax.dot_general(
+            ab[:, :, 0:128].reshape(BAND_ROWS * LONGITUDES, 128),
+            nb[:, :, cut].reshape(BAND_ROWS * LONGITUDES, columns),
+            (((0,), (0,)), ((), ())),
+            preferred_element_type=F32,
+        )
+        wg[0, 0:64, cut] = part[0:64]
+
     weights_over.wait()
-
-    @pl.loop(0, 4)
-    def _(j):
-        down_grad(j).wait()
-        up_grad(j).wait()
-
-    dkv[BAND_ROWS : BAND_ROWS + REACH, TILE:KEY_COLS, :] += hr[0].astype(F32)
-    dkv[REACH : 2 * REACH, TILE:KEY_COLS, :] += hr[1].astype(F32)
-    ab[:, TILE:LONGITUDES, 128:256] = dkv[REACH : REACH + BAND_ROWS, TILE:LONGITUDES, :].astype(BF)
-    ab[:, 0:TILE, 128:256] = dkv[REACH : REACH + BAND_ROWS, LONGITUDES:KEY_COLS, :].astype(BF)
-    kv_over = remote(ab.at[:, other_half, 128:256], asib.at[:, :, 128:256], sp.at[2], rp.at[2], sibling)
-    kv_over.start()
     oq_over.wait()
-    kv_over.wait()
-
-    def grad_part(row):
-        both = jnp.concatenate([ab[row, own_half, :], asib[row]], axis=1)
-        return jnp.dot(both, wp[...], preferred_element_type=F32)
-
-    def grad_sent(i):
-        to = (east, west, west, east, east, west)[i]
-        return remote(gs.at[i], gr.at[i], sgn.at[i], rgn.at[i], peer(to))
-
-    gs[1] = grad_part(across_opposite).astype(BF)
-    grad_sent(1).start()
-    gs[0] = grad_part(opposite).astype(BF)
-    grad_sent(0).start()
 
     low = lax.broadcasted_iota(jnp.int32, (HALF, 128), 1) < HEAD_WIDTH
 
@@ -419,8 +428,6 @@
 
     for row in (east, across_west, opposite, across_opposite):
         u_gather.arrive(row)
-
-    columns = 512
 
     @pl.loop(0, WIDTH // columns)
     def _(n):
@@ -436,57 +443,103 @@
     out_over = remote(wx.at[1 - core], wx.at[2], sp.at[3], rp.at[3], sibling)
     out_over.start()
 
+    @pl.loop(0, 8)
+    def _(j):
+        down_grad(j).wait()
+        up_grad(j).wait()
+
+    dkv[BAND_ROWS : BAND_ROWS + REACH, TILE:KEY_COLS, :] += hr[0].astype(F32)
+    dkv[REACH : 2 * REACH, TILE:KEY_COLS, :] += hr[1].astype(F32)
+    ab[:, TILE:LONGITUDES, 128:256] = dkv[REACH : REACH + BAND_ROWS, TILE:LONGITUDES, :].astype(BF)
+    ab[:, 0:TILE, 128:256] = dkv[REACH : REACH + BAND_ROWS, LONGITUDES:KEY_COLS, :].astype(BF)
+    kv_over = remote(ab.at[:, other_half, 128:256], asib.at[:, :, 128:256], sp.at[2], rp.at[2], sibling)
+    kv_over.start()
+
+    def share(b):
+        rows = pl.ds(pl.multiple_of((b // 2) * 16, 16), 16)
+        return rows, pl.ds(pl.multiple_of((b % 2) * columns, columns), columns)
+
+    def scatter(p, k):
+        rows, cut = share((lat + k) % 16)
+        return remote(wgb.at[p, rows, cut], lr.at[p, k], sl.at[p * 16 + k], rl.at[p * 16 + k], along(k))
+
+    def gather(p, k):
+        rows, cut = share(lat)
+        return remote(lf.at[p, rows, cut], lf.at[p, rows, cut], sf.at[p * 16 + k], rf.at[p * 16 + k], along(k))
+
+    def gathered(p, k):
+        rows, cut = share((lat + 16 - k) % 16)
+        return remote(lf.at[p, rows, cut], lf.at[p, rows, cut], sf.at[p * 16 + k], rf.at[p * 16 + k], along(k))
+
+    def scatter_all(p):
+        wgb[p] = wg[p].astype(BF)
+
+        @pl.loop(1, 16)
+        def _(k):
+            scatter(p, k).start()
+
+    def sum_all(p):
+        rows, cut = share(lat)
+        total = wg[p, rows, cut]
+        for k in range(1, 16):
+            scatter(p, k).wait()
+            total = total + lr[p, k].astype(F32)
+        lf[p, rows, cut] = (total * (4.0 / math.sqrt(BAND_ROWS * LONGITUDES * 16))).astype(BF)
+
+        @pl.loop(1, 16)
+        def _(k):
+            gather(p, k).start()
+
+    out_over.wait()
+    wg[0, 64:128, :] = wx[core] + wx[2]
+    scatter_all(0)
+    kv_over.wait()
+
+    def grad_part(row):
+        both = jnp.concatenate([ab[row, own_half, :], asib[row]], axis=1)
+        return jnp.dot(both, wp[...], preferred_element_type=F32)
+
+    def grad_sent(i):
+        to = (east, west, west, east, east, west)[i]
+        return remote(gs.at[i], gr.at[i], sgn.at[i], rgn.at[i], peer(to))
+
+    gs[1] = grad_part(across_opposite).astype(BF)
+    grad_sent(1).start()
+    gs[0] = grad_part(opposite).astype(BF)
+    grad_sent(0).start()
+    gs[3] = grad_part(across_east).astype(BF)
+    grad_sent(3).start()
+
     @pl.loop(0, WIDTH // columns)
     def _(n):
         cut = pl.ds(pl.multiple_of(n * columns, columns), columns)
-        part = lax.dot_general(
-            ab[...].reshape(BAND_ROWS * LONGITUDES, 256),
+        wg[1, :, cut] = lax.dot_general(
+            ab[:, :, 128:256].reshape(BAND_ROWS * LONGITUDES, 128),
             nb[:, :, cut].reshape(BAND_ROWS * LONGITUDES, columns),
             (((0,), (0,)), ((), ())),
             preferred_element_type=F32,
         )
-        wg[0:64, cut] = part[0:64]
-        wg[64:192, cut] = part[128:256]
-
-    out_over.wait()
-    wg[192:256, :] = wx[core] + wx[2]
-    wgb[...] = wg[...].astype(BF)
-
-    def share(row):
-        return pl.ds(pl.multiple_of(row * 16, 16), 16)
-
-    def scatter(k):
-        to = (lat + k) % 16
-        return remote(wgb.at[share(to)], lr.at[k], sl.at[k], rl.at[k], along(k))
-
-    def gather(k):
-        return remote(lf.at[share(lat)], lf.at[share(lat)], sf.at[k], rf.at[k], along(k))
-
-    def gathered(k):
-        row = (lat + 16 - k) % 16
-        return remote(lf.at[share(row)], lf.at[share(row)], sf.at[k], rf.at[k], along(k))
-
-    @pl.loop(1, 16)
-    def _(k):
-        scatter(k).start()
-
+
+    scatter_all(1)
+    mine[1] = grad_part(across_west)
     grad_sent(1).wait_recv()
-    gs[2] = (grad_part(across_west) + gr[1].astype(F32)).astype(BF)
+    gs[2] = (mine[1] + gr[1].astype(F32)).astype(BF)
     grad_sent(2).start()
-    gs[3] = grad_part(across_east).astype(BF)
-    grad_sent(3).start()
+    mine[0] = grad_part(east)
     grad_sent(0).wait_recv()
-    gs[4] = (grad_part(east) + gr[0].astype(F32)).astype(BF)
+    gs[4] = (mine[0] + gr[0].astype(F32)).astype(BF)
     grad_sent(4).start()
     gs[5] = grad_part(west).astype(BF)
     grad_sent(5).start()
     mine[0] = grad_part(me)
     mine[1] = grad_part(across)
+    sum_all(0)
     grad_sent(2).wait_recv()
     grad_sent(3).wait_recv()
     gy[0] = (mine[1] + gr[2].astype(F32) + gr[3].astype(F32)).astype(BF)
     over_y = remote(gy.at[0], gy.at[1], sp.at[4], rp.at[4], peer(across))
     over_y.start()
+    sum_all(1)
 
     @pl.loop(1, 8)
     def _(k):
@@ -494,16 +547,6 @@
 
     heads = jnp.concatenate([oa[k] for k in range(8)], axis=1)
     update_ref[...] = jnp.dot(heads, wall[...].reshape(WIDTH, WIDTH), preferred_element_type=F32)
-
-    total = wg[share(lat), :]
-    for k in range(1, 16):
-        scatter(k).wait()
-        total = total + lr[k].astype(F32)
-    lf[share(lat), :] = (total * (4.0 / math.sqrt(BAND_ROWS * LONGITUDES * 16))).astype(BF)
-
-    @pl.loop(1, 16)
-    def _(k):
-        gather(k).start()
 
     grad_sent(4).wait_recv()
     grad_sent(5).wait_recv()
@@ -519,9 +562,14 @@
 
     @pl.loop(1, 16)
     def _(k):
-        gather(k).wait_send()
-        gathered(k).wait_recv()
-        cotangent(k).wait_send()
+        for p in range(2):
+            gather(p, k).wait_send()
+            gathered(p, k).wait_recv()
+
+    @pl.loop(1, 8)
+    def _(k):
+        cotangent(chip(k), 0).wait_send()
+        cotangent(chip(k), 1).wait_send()
 
     grads_ref[...] = lf[...]
 
@@ -553,7 +601,7 @@
         out_shape=(
             jax.ShapeDtypeStruct((HALF, WIDTH), F32),
             jax.ShapeDtypeStruct((HALF, WIDTH), F32),
-            jax.ShapeDtypeStruct((256, WIDTH), BF),
+            jax.ShapeDtypeStruct((2, 128, WIDTH), BF),
         ),
         in_specs=[pl.BlockSpec(memory_space=VMEM)] * 5 + [pl.BlockSpec(memory_space=pltpu.SMEM)],
         out_specs=[pl.BlockSpec(memory_space=VMEM)] * 3,
@@ -581,15 +629,18 @@
             VMEM(wide, BF),
             VMEM((2, HALF, WIDTH), BF),
             VMEM((2, HALF, WIDTH), F32),
-            VMEM((256, WIDTH), F32),
-            VMEM((256, WIDTH), BF),
+            VMEM((2, 128, WIDTH), F32),
+            VMEM((2, 128, WIDTH), BF),
             VMEM((3, HEAD_WIDTH, WIDTH), F32),
-            VMEM((16, 16, WIDTH), BF),
-            VMEM((256, WIDTH), BF),
+            VMEM((2, 16, 16, WIDTH // 2), BF),
+            VMEM((2, 128, WIDTH), BF),
         ]
-        + [DMA((8,))] * 20
-        + [DMA((16,))] * 6
-        + [DMA((5,))] * 2,
+        + [DMA((8,))] * 14
+        + [DMA((16,))] * 2
+        + [DMA((8,))] * 4
+        + [DMA((16,))] * 2
+        + [DMA((32,))] * 4
+        + [DMA((6,))] * 2,
         compiler_params=pltpu.CompilerParams(
             collective_id=0, has_side_effects=True, vmem_limit_bytes=56 << 20
         ),
@@ -603,11 +654,12 @@
         row_cells,
     )
     grads = grads.astype(F32)
+    grad_qkv = jnp.concatenate([grads[0, 0:HEAD_WIDTH], grads[1]], axis=0)
     return (
         update.astype(BF),
         grad_input.astype(BF),
-        grads[0 : 3 * HEAD_WIDTH].reshape(1, 3 * HEAD_WIDTH, WIDTH),
-        grads[3 * HEAD_WIDTH :].reshape(1, HEAD_WIDTH, WIDTH),
+        grad_qkv.reshape(1, 3 * HEAD_WIDTH, WIDTH),
+        grads[0, HEAD_WIDTH:].reshape(1, HEAD_WIDTH, WIDTH),
     )
 
 

time: 125 us -> 115 us (0.920)
  Pallas kernels: 118 us -> 108 us
    pallas_call x1, Pallas kernels: 118 us -> 108 us  [on_device(): pl.pallas_call(sublayer_kernel, out_shape=(jax.ShapeDtypeStruct((HALF, WI...]
    reshape x2 -> x0, local copies, waits for them, and re-layouts: 1.66 us -> none  [the longest x1 0.93 us: on_device(): grads[0:3 * HEAD_WIDTH].reshape(1, 3 * HEAD_WIDTH, WIDTH)]
where the time goes in v5:
time: 115 us; the launch traced here: 114 us
  Pallas kernels  108 us (94%)
  other arithmetic  3.63 us (3%)
  local copies, waits for them, and re-layouts  1.18 us (1%)
    pallas_call x1, Pallas kernels, on_device(): pl.pallas_call(sublayer_kernel, out_shape=(jax.ShapeDtypeStruct((HALF, WI...  108 us

profile of v5, /device:TPU:2, one launch (start us, length us, event | category | flops | bytes accessed | tf_op | source)
XLA Modules:
  0.0 114.0 jit_solution(3927937005610648376)
XLA Ops:
  0.6 108.5 %sublayer.1 = (f32[128,1024]{1,0:T(8,128)}, f32[128,1024]{1,0:T(8,128)}, bf16[2,128,1024]{2,1,0:T(8,128)(2,1)}) custom-call(bf16[128,1024]{1,0:T(8,128)(2,1)} %tok_ref.1, f32[1,1024]{1,0:T(1,128)} %bitcast.11, bf16[192,1024]{1,0:T(8,128)(2,1)} %bitcast.9, bf16[64,1024]{1,0:T(8,128)(2,1)} %bitcast.10, bf16[128,1024]{1,0:T(8,128)(2,1)} %up_ref.1, s32[128]{0:T(128)} %cells_ref.1), custom_call_target="tpu_custom_call" | custom-call | tf_op jit(solution)/shard_map/sublayer/pallas_call | solution.py:599
  109.1 0.0 copy-start.1
  109.1 1.8 %convert_element_type.9 = bf16[128,1024]{1,0:T(8,128)(2,1)} convert(f32[128,1024]{1,0:T(8,128)} %get-tuple-element.7) | non-fusion elementwise | flops 131072 | bytes 786432 | tf_op jit(solution)/shard_map/convert_element_type | solution.py:659
  111.0 0.0 copy-done.1
  111.0 0.0 copy-start
  111.0 0.7 convert_element_type.10
  111.7 0.4 copy-done
  112.1 0.7 slice.14
  112.8 0.1 convert_element_type.11
  113.0 1.0 maximum_bitcast_fusion
  (2 shorter events, 0.1 us)
Async XLA Ops:
  109.1 1.8 %copy-start.1 = (f32[128,1024]{1,0:T(8,128)S(1)}, f32[128,1024]{1,0:T(8,128)}, u32[]{:S(2)}) copy-start(f32[128,1024]{1,0:T(8,128)} %get-tuple-element.8) | copy-start | bytes 1572868
  111.0 1.1 copy-start

commit v6 on v5

--- a/solution.py
+++ b/solution.py
@@ -115,7 +115,7 @@
     update_ref, grad_in_ref, grads_ref,
     feat, pick, nb, ub, wp, wall, kv, q, g, oq, dkv, hs, hr, ab, asib, ds, gb, os, oa, gs, gr, gy, mine, wg, wgb, wx, lr, lf,
     sn, rn, snf, rnf, su, ru, sw, rw, swf, rwf, sku, rku, skd, rkd, shg, rhg, so, ro, sgn, rgn,
-    sd, rd, sl, rl, sf, rf, sp, rp,
+    sd, rd, sl, rl, sf, rf, sp, rp, ring,
 ):
     lat, mp = lax.axis_index("lat"), lax.axis_index("mp")
     y, x, core = mp // 8, (mp // 2) % 4, mp % 2
@@ -145,10 +145,12 @@
 
     barrier = pltpu.get_barrier_semaphore()
 
-    @pl.loop(1, 16)
-    def _(k):
-        pl.semaphore_signal(barrier, inc=1, device_id={"mp": (mp + k) % 16}, device_id_type=MESH)
-        pl.semaphore_signal(barrier, inc=1, device_id=along(k), device_id_type=MESH)
+    for device in (peer(across), peer(chip(1)), peer(chip(2)), sibling, along(1), along(15)):
+        pl.semaphore_signal(barrier, inc=1, device_id=device, device_id_type=MESH)
+
+    def tell(i):
+        for step in (2**i, 16 - 2**i):
+            pl.semaphore_signal(ring.at[i], inc=1, device_id=along(step), device_id_type=MESH)
 
     def normalised():
         features = tok_ref[...].astype(F32)
@@ -162,7 +164,7 @@
     wp[0:64, :] = w_ref[0:64, :]
     wp[64:128, :] = jnp.zeros((64, WIDTH), BF)
     wp[128:256, :] = w_ref[64:192, :]
-    pl.semaphore_wait(barrier, 30)
+    pl.semaphore_wait(barrier, 6)
 
     east, west, opposite = chip(1), chip(2), chip(3)
     across_east, across_west, across_opposite = chip(5), chip(6), chip(7)
@@ -208,6 +210,7 @@
         inside = (row >= 0) & (row < 128)
         return jnp.where(inside, cells_ref[jnp.clip(row, 0, 127)], 0)
 
+    tell(0)
     dkv[...] = jnp.zeros_like(dkv)
 
     @pl.loop(0, KEY_ROWS)
@@ -281,6 +284,8 @@
     passed_on(n_gather, n_out, east, ())
     project(west)
     project(across)
+    pl.semaphore_wait(ring.at[0], 2)
+    tell(1)
     passed_on(n_gather, n_out, across_east, (6,))
     passed_on(w_gather, w_out, across_east, (6,))
     project(east)
@@ -338,6 +343,9 @@
     kv[0:REACH, LONGITUDES:KEY_COLS, :] = kv[0:REACH, 0:TILE, :]
     kv[BAND_ROWS + REACH : KEY_ROWS, LONGITUDES:KEY_COLS, :] = kv[BAND_ROWS + REACH : KEY_ROWS, 0:TILE, :]
 
+    pl.semaphore_wait(ring.at[1], 2)
+    tell(2)
+
     def halo_cut(j):
         return pl.ds(pl.multiple_of(j * WINDOW, WINDOW), WINDOW)
 
@@ -492,6 +500,7 @@
 
     out_over.wait()
     wg[0, 64:128, :] = wx[core] + wx[2]
+    pl.semaphore_wait(ring.at[2], 2)
     scatter_all(0)
     kv_over.wait()
 
@@ -640,7 +649,8 @@
         + [DMA((8,))] * 4
         + [DMA((16,))] * 2
         + [DMA((32,))] * 4
-        + [DMA((6,))] * 2,
+        + [DMA((6,))] * 2
+        + [pltpu.SemaphoreType.REGULAR((3,))],
         compiler_params=pltpu.CompilerParams(
             collective_id=0, has_side_effects=True, vmem_limit_bytes=56 << 20
         ),

time: 115 us -> 112 us (0.974)
  Pallas kernels: 108 us -> 106 us
    pallas_call x1, Pallas kernels: 108 us -> 106 us  [on_device(): pl.pallas_call(sublayer_kernel, out_shape=(jax.ShapeDtypeStruct((HALF, WI...]
where the time goes in v6:
time: 112 us; the launch traced here: 111 us
  Pallas kernels  106 us (95%)
  other arithmetic  3.63 us (3%)
  local copies, waits for them, and re-layouts  1.18 us (1%)
    pallas_call x1, Pallas kernels, on_device(): pl.pallas_call(sublayer_kernel, out_shape=(jax.ShapeDtypeStruct((HALF, WI...  106 us

profile of v6, /device:TPU:2, one launch (start us, length us, event | category | flops | bytes accessed | tf_op | source)
XLA Modules:
  0.0 111.2 jit_solution(16912627067432404319)
XLA Ops:
  0.6 105.7 %sublayer.1 = (f32[128,1024]{1,0:T(8,128)}, f32[128,1024]{1,0:T(8,128)}, bf16[2,128,1024]{2,1,0:T(8,128)(2,1)}) custom-call(bf16[128,1024]{1,0:T(8,128)(2,1)} %tok_ref.1, f32[1,1024]{1,0:T(1,128)} %bitcast.11, bf16[192,1024]{1,0:T(8,128)(2,1)} %bitcast.9, bf16[64,1024]{1,0:T(8,128)(2,1)} %bitcast.10, bf16[128,1024]{1,0:T(8,128)(2,1)} %up_ref.1, s32[128]{0:T(128)} %cells_ref.1), custom_call_target="tpu_custom_call" | custom-call | tf_op jit(solution)/shard_map/sublayer/pallas_call | solution.py:608
  106.4 0.0 copy-start.1
  106.4 1.8 %convert_element_type.9 = bf16[128,1024]{1,0:T(8,128)(2,1)} convert(f32[128,1024]{1,0:T(8,128)} %get-tuple-element.7) | non-fusion elementwise | flops 131072 | bytes 786432 | tf_op jit(solution)/shard_map/convert_element_type | solution.py:669
  108.2 0.0 copy-done.1
  108.2 0.0 copy-start
  108.2 0.7 convert_element_type.10
  109.0 0.4 copy-done
  109.3 0.7 slice.14
  110.1 0.1 convert_element_type.11
  110.3 1.0 maximum_bitcast_fusion
  (2 shorter events, 0.1 us)
Async XLA Ops:
  106.4 1.8 %copy-start.1 = (f32[128,1024]{1,0:T(8,128)S(1)}, f32[128,1024]{1,0:T(8,128)}, u32[]{:S(2)}) copy-start(f32[128,1024]{1,0:T(8,128)} %get-tuple-element.8) | copy-start | bytes 1572868
  108.2 1.1 %copy-start = (bf16[2,128,1024]{2,1,0:T(8,128)(2,1)S(1)}, bf16[2,128,1024]{2,1,0:T(8,128)(2,1)}, u32[]{:S(2)}) copy-start(bf16[2,128,1024]{2,1,0:T(8,128)(2,1)} %get-tuple-element.9) | copy-start | bytes 1572868

commit v7 on v6

--- a/solution.py
+++ b/solution.py
@@ -534,6 +534,7 @@
     grad_sent(1).wait_recv()
     gs[2] = (mine[1] + gr[1].astype(F32)).astype(BF)
     grad_sent(2).start()
+    sum_all(0)
     mine[0] = grad_part(east)
     grad_sent(0).wait_recv()
     gs[4] = (mine[0] + gr[0].astype(F32)).astype(BF)
@@ -542,7 +543,6 @@
     grad_sent(5).start()
     mine[0] = grad_part(me)
     mine[1] = grad_part(across)
-    sum_all(0)
     grad_sent(2).wait_recv()
     grad_sent(3).wait_recv()
     gy[0] = (mine[1] + gr[2].astype(F32) + gr[3].astype(F32)).astype(BF)

time: 112 us -> 112 us (level)
  no operation moved by 1% of the time
where the time goes in v7:
time: 112 us; the launch traced here: 111 us
  Pallas kernels  106 us (95%)
  other arithmetic  3.63 us (3%)
  local copies, waits for them, and re-layouts  1.18 us (1%)
    pallas_call x1, Pallas kernels, on_device(): pl.pallas_call(sublayer_kernel, out_shape=(jax.ShapeDtypeStruct((HALF, WI...  106 us

profile of v7, /device:TPU:2, one launch (start us, length us, event | category | flops | bytes accessed | tf_op | source)
XLA Modules:
  0.0 111.1 jit_solution(3366682580933412641)
XLA Ops:
  0.6 105.6 %sublayer.1 = (f32[128,1024]{1,0:T(8,128)}, f32[128,1024]{1,0:T(8,128)}, bf16[2,128,1024]{2,1,0:T(8,128)(2,1)}) custom-call(bf16[128,1024]{1,0:T(8,128)(2,1)} %tok_ref.1, f32[1,1024]{1,0:T(1,128)} %bitcast.11, bf16[192,1024]{1,0:T(8,128)(2,1)} %bitcast.9, bf16[64,1024]{1,0:T(8,128)(2,1)} %bitcast.10, bf16[128,1024]{1,0:T(8,128)(2,1)} %up_ref.1, s32[128]{0:T(128)} %cells_ref.1), custom_call_target="tpu_custom_call" | custom-call | tf_op jit(solution)/shard_map/sublayer/pallas_call | solution.py:608
  106.2 0.0 copy-start.1
  106.2 1.8 %convert_element_type.9 = bf16[128,1024]{1,0:T(8,128)(2,1)} convert(f32[128,1024]{1,0:T(8,128)} %get-tuple-element.7) | non-fusion elementwise | flops 131072 | bytes 786432 | tf_op jit(solution)/shard_map/convert_element_type | solution.py:669
  108.1 0.0 copy-done.1
  108.1 0.0 copy-start
  108.1 0.7 convert_element_type.10
  108.8 0.4 copy-done
  109.2 0.7 slice.14
  109.9 0.1 convert_element_type.11
  110.1 1.0 maximum_bitcast_fusion
  (2 shorter events, 0.1 us)
Async XLA Ops:
  106.2 1.8 %copy-start.1 = (f32[128,1024]{1,0:T(8,128)S(1)}, f32[128,1024]{1,0:T(8,128)}, u32[]{:S(2)}) copy-start(f32[128,1024]{1,0:T(8,128)} %get-tuple-element.8) | copy-start | bytes 1572868
  108.1 1.1 %copy-start = (bf16[2,128,1024]{2,1,0:T(8,128)(2,1)S(1)}, bf16[2,128,1024]{2,1,0:T(8,128)(2,1)}, u32[]{:S(2)}) copy-start(bf16[2,128,1024]{2,1,0:T(8,128)(2,1)} %get-tuple-element.9) | copy-start | bytes 1572868
